TPU v7x, 256 devices: a whole 4x4x8 slice. The times are simulated.
256 devices in a mesh: qrow: 8 (over x, z_lo), kcol: 32 (over y, z_hi, core).
Axes of the slice: x: 4, y: 4, z: 8 (z_hi: 4, z_lo: 2; z = z_hi * 2 + z_lo), core: 2. Of those that a mesh axis runs over, the one named last changes fastest.
Arguments:
- queries: bfloat16 [256, 2048], P(('qrow', 'kcol')), may hold values from -96 to 96, as said below
- key_maps: bfloat16 [65536, 2048], P(('qrow', 'kcol')), may hold values from -4.1 to 4.1, as said below
- values: bfloat16 [65536, 2048], P(('qrow', 'kcol')), may hold values from -24 to 24
- lambdas: float32 [8], replicated, may hold values from 0.2 to 0.8
- norm_gain: float32 [2048], replicated, may hold values from 0.1 to 1.9
Outputs:
- attended: bfloat16 [256, 2048], P(('qrow', 'kcol'))
Inputs may be any that keep to these rules, and one draw needn't show every extreme that they name: `queries`: query features of order one in most rows. `key_maps`: key features of order one.
All inputs are finite; a program needn't handle non-finite values.
Results may differ from a plain program's by a relative error of at most 0.014.
Values may be sent and summed in bfloat16 or wider, within the bound.
No kernel may reach another device: no remote copies, remote signals or barrier semaphores. Data moves between devices by JAX's collectives and lax.ppermute only.
A program may use at most 64 MiB of HBM per device.

v0:
```python
import math

import jax
import jax.numpy as jnp
from jax import lax
from jax.sharding import PartitionSpec as P


def combined_all(array, axis, combine):
    everything = jax.tree.map(lambda part: lax.all_gather(part, axis), array)
    leading = jax.tree.map(lambda part: part[0], everything)

    def lap(k, so_far):
        return combine(so_far, jax.tree.map(lambda part: part[k], everything))

    return lax.fori_loop(1, lax.axis_size(axis), lap, leading)


def combine_states(first, second):
    max_one, total_one, accum_one = first
    max_two, total_two, accum_two = second
    largest = jnp.maximum(max_one, max_two)
    factor_one = jnp.exp(max_one - largest)
    factor_two = jnp.exp(max_two - largest)
    totals = total_one * factor_one + total_two * factor_two
    accums = accum_one * factor_one[..., None] + accum_two * factor_two[..., None]
    return (largest, totals, accums)


def shards(queries, key_maps, values, lambdas, norm_gain):
    row_count = lax.axis_size("qrow")
    col_count = lax.axis_size("kcol")
    row_index = lax.axis_index("qrow")
    col_index = lax.axis_index("kcol")
    query_dev = queries.shape[0]
    key_dev = key_maps.shape[0]
    head_count = lambdas.shape[0]
    head_width = key_maps.shape[1] // (2 * head_count)
    value_width = values.shape[1] // head_count
    total_keys = key_dev * row_count * col_count
    total_queries = query_dev * row_count * col_count
    scaling = 1.0 / math.sqrt(head_width)
    row_block = lax.all_gather(queries, "kcol", axis=0, tiled=True)
    row_size = row_block.shape[0]
    query_pos = (
        total_keys - total_queries + row_index * row_size + jnp.arange(row_size, dtype=jnp.int32)
    )
    run_max = jnp.full((2, row_size, head_count), -1e30, jnp.float32)
    key_piece = lax.all_gather(key_maps, "qrow", axis=0, tiled=True)
    value_piece = lax.all_gather(values, "qrow", axis=0, tiled=True)
    count = key_piece.shape[0]
    global_row = jnp.arange(count, dtype=jnp.int32)
    key_pos = (global_row // key_dev * col_count + col_index) * key_dev + global_row % key_dev
    visible = key_pos[None, :] <= query_pos[:, None]
    new_max = []
    new_total = []
    new_accum = []
    for map_side in range(2):
        side_max, side_total, side_accum = ([], [], [])
        for head_index in range(head_count):
            lower = (head_index * 2 + map_side) * head_width
            score = (
                lax.dot_general(
                    row_block[:, lower : lower + head_width],
                    key_piece[:, lower : lower + head_width],
                    (((1,), (1,)), ((), ())),
                    preferred_element_type=jnp.float32,
                )
                * scaling
            )
            score = jnp.where(visible, score, -1e30)
            before = run_max[map_side, :, head_index]
            largest = jnp.maximum(before, jnp.max(score, axis=1))
            expo = jnp.where(visible, jnp.exp(score - largest[:, None]), 0.0)
            side_total.append(jnp.sum(expo, axis=1))
            product = jnp.dot(
                expo.astype(jnp.bfloat16),
                value_piece[:, head_index * value_width : (head_index + 1) * value_width],
                preferred_element_type=jnp.float32,
            )
            side_accum.append(product)
            side_max.append(largest)
        new_max.append(jnp.stack(side_max, axis=1))
        new_total.append(jnp.stack(side_total, axis=1))
        new_accum.append(jnp.stack(side_accum, axis=1))
    part_max = jnp.stack(new_max)
    part_total = jnp.stack(new_total)
    part_accum = jnp.stack(new_accum)
    merged = combined_all((part_max, part_total, part_accum), "kcol", combine_states)
    outputs = merged[2] / merged[1][..., None]
    whole_diff = outputs[0] - lambdas[None, :, None] * outputs[1]
    own_diff = lax.dynamic_slice_in_dim(whole_diff, col_index * query_dev, query_dev, 0)
    meansq = jnp.mean(own_diff * own_diff, axis=-1, keepdims=True)
    normed = own_diff / jnp.sqrt(meansq + 1e-05) * norm_gain.reshape(head_count, value_width)
    return normed.reshape(query_dev, head_count * value_width).astype(jnp.bfloat16)


def solution(mesh):
    in_specs = (
        P(("qrow", "kcol"), None),
        P(("qrow", "kcol"), None),
        P(("qrow", "kcol"), None),
        P(),
        P(),
    )
    out_specs = P(("qrow", "kcol"), None)
    return jax.shard_map(shards, mesh=mesh, in_specs=in_specs, out_specs=out_specs, check_vma=False)
```

profile of v0, /device:TPU:32, one launch (start us, length us, event | category | flops | bytes accessed | tf_op | source)
XLA Modules:
  0.0 551.5 jit_solution(6906678680152131153)
XLA Ops:
  8.1 48.4 %all-gather.3 = bf16[32,1,2048]{2,1,0:T(2,128)(2,1)S(1)} all-gather(bf16[1,1,2048]{2,1,0:T(2,128)(2,1)} %bitcast.176), channel_id=1, replica_groups=mesh['qrow'=8,'kcol'=32] {'kcol'}, dimensions={0}, use_global_device_ids=true | all-gather | bytes 135168 | tf_op jit(solution)/shard_map/all_gather | solution.py:43
  57.2 127.4 %all-gather.8.cloned.1.call-done = bf16[2048,2048]{1,0:T(8,128)(2,1)} async-done(((bf16[256,2048]{1,0:T(8,128)(2,1)}), bf16[2048,2048]{1,0:T(8,128)(2,1)}) %all-gather.8.cloned.1.call-update) | async-done | bytes 8388624 | tf_op jit(solution)/shard_map/all_gather | solution.py:49
  186.1 1.5 fusion.224
  189.0 1.5 fusion.226
  191.9 1.5 fusion.228
  194.8 1.5 fusion.230
  197.8 1.5 fusion.232
  200.7 1.5 fusion.234
  202.2 2.3 fusion.237
  204.5 2.2 fusion.236
  207.2 1.5 fusion.239
  208.7 2.2 fusion.238
  211.5 146.4 %all-gather.10.cloned.1.call-done = bf16[2048,2048]{1,0:T(8,128)(2,1)} async-done(((bf16[256,2048]{1,0:T(8,128)(2,1)}), bf16[2048,2048]{1,0:T(8,128)(2,1)}) %all-gather.10.cloned.1.call-update) | async-done | bytes 8388624 | tf_op jit(solution)/shard_map/all_gather | solution.py:50
  357.9 1.7 fusion.10
  359.6 2.3 fusion.18
  361.9 1.6 fusion.9
  363.5 1.6 fusion.8
  365.1 1.6 fusion.7
  366.7 1.6 fusion.6
  373.7 47.0 %all-gather = f32[64,32,8]{1,2,0:T(8,128)S(1)} all-gather(f32[2,32,8]{1,2,0:T(8,128)S(1)} %pad_maximum_fusion.1), channel_id=2, replica_groups=mesh['qrow'=8,'kcol'=32] {'kcol'}, dimensions={0}, use_global_device_ids=true | all-gather | bytes 67584 | tf_op jit(solution)/shard_map/all_gather | solution.py:10
  420.7 2.1 fusion.64
  423.5 63.1 %all-gather.1 = f32[64,32,8]{1,2,0:T(8,128)S(1)} all-gather(f32[2,32,8]{1,2,0:T(8,128)S(1)} %pad_maximum_fusion.2), channel_id=3, replica_groups=mesh['qrow'=8,'kcol'=32] {'kcol'}, dimensions={0}, use_global_device_ids=true | all-gather | bytes 67584 | tf_op jit(solution)/shard_map/all_gather | solution.py:10
  486.6 9.7 %all-gather.12.cloned.1.call-done = f32[64,32,8,256]{3,2,1,0:T(8,128)} async-done(((f32[2,32,8,256]{3,2,1,0:T(8,128)}), f32[64,32,8,256]{3,2,1,0:T(8,128)}) %all-gather.12.cloned.1.call-update) | async-done | bytes 16777232 | tf_op jit(solution)/shard_map/all_gather | solution.py:10
  497.3 46.5 %while.19 = (s32[]{:T(128)}, f32[2,32,8]{1,2,0:T(8,128)S(1)}, f32[2,32,8]{1,2,0:T(8,128)S(1)}, f32[2,32,8,256]{3,2,1,0:T(8,128)S(1)}, f32[32,2,32,8]{2,3,1,0:T(8...) while((s32[]{:T(128)}, f32[2,32,8]{1,2,0:T(8,128)S(1)}, ...), condition=%wide.region_33.34_spmd, body=%wide.region_32.33_spmd.sunk | while | flops 396293 | bytes 1601687 | solution.py:16
  (191 shorter events, 65.8 us)
Async XLA Ops:
  6.5 178.1 %all-gather.8.cloned.1.call-start = ((), (), s32[]{:S(2)}) async-start(), calls=%async_computation | async-start | bytes 9437184 | tf_op jit(solution)/shard_map/all_gather | solution.py:49
  7.3 350.6 %all-gather.10.cloned.1.call-start = ((), (), s32[]{:S(2)}) async-start(), calls=%async_computation.1 | async-start | bytes 9437184 | tf_op jit(solution)/shard_map/all_gather | solution.py:50
  8.0 488.2 %all-gather.12.cloned.1.call-start = ((), (), s32[]{:S(2)}) async-start(), calls=%async_computation.2 | async-start | bytes 17301504 | tf_op jit(solution)/shard_map/all_gather | solution.py:10
  202.2 167.5 %copy-start = (f32[32,2048]{1,0:T(8,128)}, f32[32,2048]{1,0:T(8,128)S(1)}, u32[]{:S(2)}) copy-start(f32[32,2048]{1,0:T(8,128)S(1)} %get-tuple-element.287) | copy-start | bytes 786436
  357.9 10.4 %copy-start.6 = (bf16[2048,2048]{1,0:T(8,128)(2,1)S(1)}, bf16[2048,2048]{1,0:T(8,128)(2,1)}, u32[]{:S(2)}) copy-start(bf16[2048,2048]{1,0:T(8,128)(2,1)} %all-gather.10.cloned.1.call-done) | copy-start | bytes 25165828
  359.6 10.8 %copy-start.2 = (f32[32,2048]{1,0:T(8,128)S(1)}, f32[32,2048]{1,0:T(8,128)}, u32[]{:S(2)}) copy-start(f32[32,2048]{1,0:T(8,128)} %get-tuple-element.291) | copy-start | bytes 786436
  361.9 8.8 %copy-start.1 = (f32[32,2048]{1,0:T(8,128)S(1)}, f32[32,2048]{1,0:T(8,128)}, u32[]{:S(2)}) copy-start(f32[32,2048]{1,0:T(8,128)} %get-tuple-element.293) | copy-start | bytes 786436
  363.5 7.5 %copy-start.3 = (f32[32,2048]{1,0:T(8,128)S(1)}, f32[32,2048]{1,0:T(8,128)}, u32[]{:S(2)}) copy-start(f32[32,2048]{1,0:T(8,128)} %get-tuple-element.295) | copy-start | bytes 786436
  368.6 4.3 copy-start.4
  420.7 123.4 %copy-start.5 = (f32[8]{0:T(128)S(1)}, f32[8]{0:T(128)}, u32[]{:S(2)}) copy-start(f32[8]{0:T(128)} %param.10) | copy-start | bytes 100
Sparse Core Ops, SparseCore 0:
  9.1 175.4 all-gather.7
  186.4 171.4 all-gather.9
  373.1 123.1 all-gather.11
where the time goes:
time: 555 us; the launch traced here: 551 us
  waiting for transfers between devices  285 us (51%)
  blocking collectives  159 us (29%)
  other arithmetic  45.2 us (8%)
  matrix products  39.3 us (7%)
  between operations  13.4 us (2%)
  local copies, waits for them, and re-layouts  9.21 us (2%)
    all_gather x1, waiting for transfers between devices, shards(): value_piece = lax.all_gather(values, 'qrow', axis=0, tiled=True)  146 us
    all_gather x1, waiting for transfers between devices, shards(): key_piece = lax.all_gather(key_maps, 'qrow', axis=0, tiled=True)  127 us
    all_gather x2, blocking collectives, combined_all(): everything = jax.tree.map(lambda part: lax.all_gather(part, axis), array)  110 us
    all_gather x1, blocking collectives, shards(): row_block = lax.all_gather(queries, 'kcol', axis=0, tiled=True)  48.4 us
    add x31, other arithmetic, combine_states(): accum_one * factor_one[..., None] + accum_two * factor_two[..., None]  40.1 us
    dot_general x16, matrix products, shards(): lax.dot_general(row_block[:, lower:lower + head_width], key_piece[:, lowe...  25.5 us
    dot_general x16, matrix products, shards(): jnp.dot(expo.astype(jnp.bfloat16), value_piece[:, head_index * value_widt...  13.7 us
  transfers between devices with their start and end apart: 3, of which 3 were waited for; matrix products, arithmetic and copies ran while one was open for 6% of the time, Pallas kernels for 0%

commit v1 on v0

v1 whole, which is shorter than its diff:
```python
import functools
import math

import jax
import jax.numpy as jnp
from jax import lax
from jax.experimental import pallas as pl
from jax.experimental.pallas import tpu as pltpu
from jax.sharding import Mesh, PartitionSpec as P

HEADS = 8
MAPS = 16
HD = 128
VD = 256
KEYS = 256
DEVICES = 256
CHIPS = 128
PLANE = 16
COLUMN = 8
SUMS = MAPS * VD
WIDE = SUMS + 128
NEG = -1e30
AXES = ("x", "z_lo", "y", "z_hi", "core")
BF16 = jnp.bfloat16
F32 = jnp.float32


def attend(place_ref, q_ref, ka_ref, va_ref, kb_ref, vb_ref, out_ref, stats_ref):
    head = pl.program_id(0)
    place = place_ref[0]
    core = place % 2
    row = lax.broadcasted_iota(jnp.int32, (CHIPS, KEYS), 0)
    device = (row // 32) * 64 + ((row // 4) % 2) * 32 + ((row // 8) % 4) * 8 + (row % 4) * 2 + core
    ahead = device - lax.broadcasted_iota(jnp.int32, (CHIPS, KEYS), 1) + (DEVICES - 1) * KEYS
    seen_a = ahead >= place * KEYS
    seen_b = ahead >= (place + 1 - 2 * core) * KEYS
    scaling = math.log2(math.e) / math.sqrt(HD)
    lane = lax.broadcasted_iota(jnp.int32, (CHIPS, 128), 1)
    trans = (((1,), (1,)), ((), ()))

    @pl.when(head == 0)
    def _():
        stats_ref[...] = jnp.zeros_like(stats_ref)

    stats = stats_ref[...]
    for side in range(2):
        cols = slice(side * HD, (side + 1) * HD)
        q = q_ref[:, cols]
        sa = lax.dot_general(q, ka_ref[:, cols], trans, preferred_element_type=F32) * scaling
        sb = lax.dot_general(q, kb_ref[:, cols], trans, preferred_element_type=F32) * scaling
        sa = jnp.where(seen_a, sa, NEG)
        sb = jnp.where(seen_b, sb, NEG)
        top = jnp.max(jnp.maximum(sa, sb), axis=1, keepdims=True).astype(BF16).astype(F32)
        ea = jnp.exp2(sa - top)
        eb = jnp.exp2(sb - top)
        total = jnp.sum(ea + eb, axis=1, keepdims=True)
        acc = jnp.dot(ea.astype(BF16), va_ref[...], preferred_element_type=F32)
        acc += jnp.dot(eb.astype(BF16), vb_ref[...], preferred_element_type=F32)
        index = head * 2 + side
        out_ref[:, pl.ds(pl.multiple_of(index * VD, VD), VD)] = acc.astype(BF16)
        high = total.astype(BF16).astype(F32)
        stats = jnp.where(lane == index, top, stats)
        stats = jnp.where(lane == index + MAPS, high, stats)
        stats = jnp.where(lane == index + 2 * MAPS, total - high, stats)
    stats_ref[...] = stats

    @pl.when(head == HEADS - 1)
    def _():
        out_ref[:, SUMS:] = stats.astype(BF16)


def merge_plane(in_ref, out_ref):
    stats = in_ref[:, SUMS:].astype(F32)
    total = pltpu.roll(stats, 128 - MAPS, 1) + pltpu.roll(stats, 128 - 2 * MAPS, 1)
    stats = stats.reshape(PLANE, COLUMN, 128)
    total = total.reshape(PLANE, COLUMN, 128)
    top = jnp.max(stats, axis=0)
    weight = jnp.exp2(stats - top[None])
    total = jnp.sum(weight * total, axis=0)
    lane = lax.broadcasted_iota(jnp.int32, (COLUMN, 128), 1)
    out_ref[:, SUMS:] = jnp.where(lane < MAPS, top, pltpu.roll(total, MAPS, 1))
    for index in range(MAPS):
        cols = slice(index * VD, (index + 1) * VD)
        part = in_ref[:, cols].astype(F32).reshape(PLANE, COLUMN, VD)
        out_ref[:, cols] = jnp.sum(part * weight[:, :, index : index + 1], axis=0)


def merge_column(lam_ref, in_ref, gain_ref, out_ref):
    stats = in_ref[:, SUMS:]
    total = pltpu.roll(stats, 128 - MAPS, 1)
    top = jnp.max(stats, axis=0, keepdims=True)
    weight = jnp.exp2(stats - top)
    lane = lax.broadcasted_iota(jnp.int32, (COLUMN, 128), 1)
    total = jnp.where(lane < MAPS, jnp.sum(weight * total, axis=0, keepdims=True), 1.0)
    weight = weight / total
    for head in range(HEADS):
        outs = []
        for index in (2 * head, 2 * head + 1):
            part = in_ref[:, index * VD : (index + 1) * VD]
            outs.append(jnp.sum(part * weight[:, index : index + 1], axis=0, keepdims=True))
        diff = outs[0] - lam_ref[head] * outs[1]
        meansq = jnp.mean(diff * diff, axis=1, keepdims=True)
        cols = slice(head * VD, (head + 1) * VD)
        out_ref[:, cols] = (diff / jnp.sqrt(meansq + 1e-5) * gain_ref[:, cols]).astype(BF16)


def shards(queries, key_maps, values, lambdas, norm_gain):
    swap = [(0, 1), (1, 0)]
    key_other = lax.ppermute(key_maps, "core", swap)
    value_other = lax.ppermute(values, "core", swap)
    place = lax.axis_index(AXES).astype(jnp.int32).reshape(1)

    spread = jnp.broadcast_to(queries.reshape(1, MAPS, HD), (COLUMN, MAPS, HD))
    column = lax.all_to_all(spread, ("z_lo", "z_hi"), 0, 0, tiled=True)
    column = column.reshape(1, COLUMN, MAPS * HD)
    spread = jnp.broadcast_to(column, (PLANE, COLUMN, MAPS * HD))
    q_all = lax.all_to_all(spread, ("x", "y"), 0, 0, tiled=True).reshape(CHIPS, MAPS * HD)

    per_head = pl.BlockSpec((KEYS, 2 * HD), lambda h: (0, h))
    partial = pl.pallas_call(
        attend,
        grid=(HEADS,),
        in_specs=[
            pl.BlockSpec(memory_space=pltpu.SMEM),
            pl.BlockSpec((CHIPS, 2 * HD), lambda h: (0, h)),
            per_head,
            per_head,
            per_head,
            per_head,
        ],
        out_specs=pl.BlockSpec((CHIPS, WIDE), lambda h: (0, 0)),
        out_shape=jax.ShapeDtypeStruct((CHIPS, WIDE), BF16),
        scratch_shapes=[pltpu.VMEM((CHIPS, 128), F32)],
        name="attend",
    )(place, q_all, key_maps, values, key_other, value_other)

    partial = partial.reshape(PLANE, COLUMN, WIDE)
    partial = lax.all_to_all(partial, ("x", "y"), 0, 0, tiled=True)
    merged = pl.pallas_call(
        merge_plane,
        out_shape=jax.ShapeDtypeStruct((COLUMN, WIDE), F32),
        name="merge_plane",
    )(partial.reshape(CHIPS, WIDE))
    merged = lax.all_to_all(merged, ("z_lo", "z_hi"), 0, 0, tiled=True)
    vmem = pl.BlockSpec(memory_space=pltpu.VMEM)
    return pl.pallas_call(
        merge_column,
        in_specs=[pl.BlockSpec(memory_space=pltpu.SMEM), vmem, vmem],
        out_specs=vmem,
        out_shape=jax.ShapeDtypeStruct((1, HEADS * VD), BF16),
        name="merge_column",
    )(lambdas, merged, norm_gain.reshape(1, HEADS * VD))


def solution(mesh):
    fine = Mesh(mesh.devices.reshape(4, 2, 4, 4, 2), AXES)
    rows = P(AXES, None)
    return jax.shard_map(
        shards,
        mesh=fine,
        in_specs=(rows, rows, rows, P(), P()),
        out_specs=rows,
        check_vma=False,
    )
```

time: 555 us -> 81.6 us (0.15)
  waiting for transfers between devices: 285 us -> 10.2 us
  blocking collectives: 159 us -> 45.8 us
  other arithmetic: 45.2 us -> 0.73 us
  matrix products: 39.3 us -> 0 us
  between operations: 13.4 us -> 0.05 us
  Pallas kernels: 0 us -> 12.6 us
  starting transfers between devices: 0.08 us -> 7.54 us
    all_gather x3 -> x0, waiting for transfers between devices: 283 us -> none  [the longest x1 146 us: shards(): value_piece = lax.all_gather(values, 'qrow', axis=0, tiled=True)]
    all_gather x3 -> x0, blocking collectives: 159 us -> none  [the longest x2 110 us: combined_all(): everything = jax.tree.map(lambda part: lax.all_gather(part, axis), array)]
    all_to_all x0 -> x3, blocking collectives: none -> 45.8 us  [the longest x1 19.7 us: shards(): partial = lax.all_to_all(partial, ('x', 'y'), 0, 0, tiled=True)]
    add x64 -> x0, other arithmetic: 40.7 us -> none  [the longest x31 40.1 us: combine_states(): accum_one * factor_one[..., None] + accum_two * factor_two[..., None]]
    dot_general x32 -> x0, matrix products: 39.3 us -> none  [the longest x16 25.5 us: shards(): lax.dot_general(row_block[:, lower:lower + head_width], key_piece[:, lowe...]
    pallas_call x0 -> x3, Pallas kernels: none -> 12.6 us  [the longest x1 8.57 us: shards(): pl.pallas_call(attend, grid=(HEADS,), in_specs=[pl.BlockSpec(memory_space...]
    all_to_all x0 -> x1, waiting for transfers between devices: none -> 10.2 us  [shards(): lax.all_to_all(spread, ('x', 'y'), 0, 0, tiled=True)]
    all_to_all x0 -> x1, starting transfers between devices: none -> 7.03 us  [shards(): lax.all_to_all(spread, ('x', 'y'), 0, 0, tiled=True)]
  transfers between devices with their start and end apart: 3 -> 3, of which waited for: 3 -> 1; matrix products, arithmetic and copies ran while one was open for 6% -> 2% of each run, Pallas kernels for 0% -> 0%
where the time goes in v1:
time: 81.6 us; the launch traced here: 81.1 us
  blocking collectives  45.8 us (56%)
  Pallas kernels  12.6 us (15%)
  waiting for transfers between devices  10.2 us (12%)
  starting transfers between devices  7.54 us (9%)
  local copies, waits for them, and re-layouts  4.05 us (5%)
    all_to_all x1, blocking collectives, shards(): partial = lax.all_to_all(partial, ('x', 'y'), 0, 0, tiled=True)  19.7 us
    all_to_all x1, blocking collectives, shards(): column = lax.all_to_all(spread, ('z_lo', 'z_hi'), 0, 0, tiled=True)  14.9 us
    all_to_all x1, blocking collectives, shards(): merged = lax.all_to_all(merged, ('z_lo', 'z_hi'), 0, 0, tiled=True)  11.2 us
    all_to_all x1, waiting for transfers between devices, shards(): lax.all_to_all(spread, ('x', 'y'), 0, 0, tiled=True)  10.2 us
    pallas_call x1, Pallas kernels, shards(): pl.pallas_call(attend, grid=(HEADS,), in_specs=[pl.BlockSpec(memory_space...  8.57 us
    all_to_all x1, starting transfers between devices, shards(): lax.all_to_all(spread, ('x', 'y'), 0, 0, tiled=True)  7.03 us
    pallas_call x1, Pallas kernels, shards(): pl.pallas_call(merge_plane, out_shape=jax.ShapeDtypeStruct((COLUMN, WIDE)...  2.27 us
    unnamed x8, local copies, waits for them, and re-layouts  2.15 us
  transfers between devices with their start and end apart: 3, of which 1 were waited for; matrix products, arithmetic and copies ran while one was open for 2% of the time, Pallas kernels for 0%

profile of v1, /device:TPU:32, one launch (start us, length us, event | category | flops | bytes accessed | tf_op | source)
XLA Modules:
  0.0 81.1 jit_solution(11736144920714647604)
XLA Ops:
  0.0 0.0 collective-permute-start
  0.0 0.5 collective-permute-start.1
  0.5 0.7 reduce
  1.3 14.9 %all_to_all.26 = bf16[8,16,128]{2,1,0:T(8,128)(2,1)S(1)} all-to-all(bf16[8,16,128]{2,1,0:T(8,128)(2,1)S(1)} %broadcast_in_dim.15), channel_id=1, replica_groups=mesh['x'=4,'z_lo'=2,'y'=4,'z_hi'=4,'core'=2] {'z_lo','z_hi'}, dimensions={0} | all-to-all | bytes 65536 | tf_op jit(solution)/shard_map/all_to_all | solution.py:114
  16.2 0.8 %broadcast_in_dim.17 = bf16[16,8,2048]{2,1,0:T(8,128)(2,1)} broadcast(bf16[8,2048]{1,0:T(8,128)(2,1)S(1)} %bitcast.19), dimensions={1,2} | broadcast | bytes 557056 | tf_op jit(solution)/shard_map/broadcast_in_dim | solution.py:116
  17.0 7.0 %all-to-all-start.1 = ((bf16[16,8,2048]{2,1,0:T(8,128)(2,1)}), bf16[16,8,2048]{2,1,0:T(8,128)(2,1)S(1)}, u32[]{:S(2)}, u32[]{:S(2)}) async-start(bf16[16,8,2048]{2,1,0:T(8,128)(2,1)} %broadcast_in_dim.17), calls=%async_computation.1 | async-start | bytes 1048576 | tf_op jit(solution)/shard_map/all_to_all | solution.py:117
  24.1 10.2 %all-to-all-done.1 = bf16[16,8,2048]{2,1,0:T(8,128)(2,1)S(1)} async-done(((bf16[16,8,2048]{2,1,0:T(8,128)(2,1)}), bf16[16,8,2048]{2,1,0:T(8,128)(2,1)S(1)}, u32[]{:S(2)}, u32[]{:S(2)}) %all-to-all-start.1) | async-done | bytes 524320 | tf_op jit(solution)/shard_map/all_to_all | solution.py:117
  34.3 0.0 copy-start
  34.3 0.0 collective-permute-done.kb_ref
  34.3 0.0 copy-start.1
  34.3 0.0 collective-permute-done.1.vb_ref
  34.3 0.0 copy-start.2
  34.3 0.8 copy-done
  35.1 0.4 copy-done.1
  35.5 0.3 copy-done.2
  35.8 8.6 %attend.1 = bf16[128,4224]{1,0:T(8,128)(2,1)} custom-call(s32[1]{0:T(128)} %bitcast.place_ref, bf16[128,2048]{1,0:T(8,128)(2,1)} %bitcast.16, bf16[256,2048]{1,0:T(8,128)(2,1)} %ka_ref.1, bf16[256,2048]{1,0:T(8,128)(2,1)} %va_ref.1, bf16[256,2048]{1,0:T(8,128)(2,1)} %copy-done.1, bf16[256,2048]{1,0:T(8,128)(2,1)} %copy-done.2), custom_call_target="tpu_custom_call" | custom-call | tf_op jit(solution)/shard_map/attend/pallas_call | solution.py:120
  44.4 19.7 %all_to_all.27 = bf16[16,8,4224]{2,1,0:T(8,128)(2,1)} all-to-all(bf16[16,8,4224]{2,1,0:T(8,128)(2,1)} %bitcast.15), channel_id=1, replica_groups=mesh['x'=4,'z_lo'=2,'y'=4,'z_hi'=4,'core'=2] {'x','y'}, dimensions={0} | all-to-all | bytes 2162688 | tf_op jit(solution)/shard_map/all_to_all | solution.py:138
  64.1 2.3 %merge_plane.1 = f32[8,4224]{1,0:T(8,128)} custom-call(bf16[128,4224]{1,0:T(8,128)(2,1)} %bitcast.14), custom_call_target="tpu_custom_call" | custom-call | tf_op jit(solution)/shard_map/merge_plane/pallas_call | solution.py:139
  66.4 1.0 %copy.6 = f32[8,1,4224]{2,1,0:T(1,128)S(1)} copy(f32[8,1,4224]{2,0,1:T(8,128)} %bitcast.17) | data formatting | bytes 270336 | tf_op jit(solution)/shard_map/all_to_all | solution.py:144
  67.4 11.2 %all_to_all.28 = f32[8,1,4224]{2,1,0:T(1,128)S(1)} all-to-all(f32[8,1,4224]{2,1,0:T(1,128)S(1)} %copy.6), channel_id=1, replica_groups=mesh['x'=4,'z_lo'=2,'y'=4,'z_hi'=4,'core'=2] {'z_lo','z_hi'}, dimensions={0} | all-to-all | bytes 270336 | tf_op jit(solution)/shard_map/all_to_all | solution.py:144
  78.6 0.7 copy.11
  79.3 1.8 %merge_column.1 = bf16[1,2048]{1,0:T(2,128)(2,1)} custom-call(f32[8]{0:T(128)} %lam_ref.1, f32[8,4224]{1,0:T(8,128)} %bitcast.18, f32[1,2048]{1,0:T(1,128)} %bitcast.22), custom_call_target="tpu_custom_call" | custom-call | tf_op jit(solution)/shard_map/merge_column/pallas_call | solution.py:146
  (2 shorter events, 0.0 us)
Async XLA Ops:
  0.0 34.3 %collective-permute-start = (bf16[256,2048]{1,0:T(8,128)(2,1)}, bf16[256,2048]{1,0:T(8,128)(2,1)S(1)}, u32[]{:S(2)}, u32[]{:S(2)}) collective-permute-start(bf16[256,2048]{1,0:T(8,128)(2,1)} %ka_ref.1), channel_id=1, source_target_pairs={{0,1},{1,0},{2,3},{3,2},{4,5},{5,4},{6,7},{7,6},{8,9},{9,8},{10,11... | collective-permute-start | bytes 3145736 | tf_op jit(solution)/shard_map/ppermute | solution.py:109
  0.0 34.3 %collective-permute-start.1 = (bf16[256,2048]{1,0:T(8,128)(2,1)}, bf16[256,2048]{1,0:T(8,128)(2,1)S(1)}, u32[]{:S(2)}, u32[]{:S(2)}) collective-permute-start(bf16[256,2048]{1,0:T(8,128)(2,1)} %va_ref.1), channel_id=1, source_target_pairs={{0,1},{1,0},{2,3},{3,2},{4,5},{5,4},{6,7},{7,6},{8,9},{9,8},{10,11... | collective-permute-start | bytes 3145736 | tf_op jit(solution)/shard_map/ppermute | solution.py:110
  17.0 17.3 %all-to-all-start.1 = ((bf16[16,8,2048]{2,1,0:T(8,128)(2,1)}), bf16[16,8,2048]{2,1,0:T(8,128)(2,1)S(1)}, u32[]{:S(2)}, u32[]{:S(2)}) async-start(bf16[16,8,2048]{2,1,0:T(8,128)(2,1)} %broadcast_in_dim.17), calls=%async_computation.1 | async-start | bytes 1048576 | tf_op jit(solution)/shard_map/all_to_all | solution.py:117
  34.3 0.8 copy-start
  34.3 1.2 %copy-start.1 = (bf16[256,2048]{1,0:T(8,128)(2,1)}, bf16[256,2048]{1,0:T(8,128)(2,1)S(1)}, u32[]{:S(2)}) copy-start(bf16[256,2048]{1,0:T(8,128)(2,1)S(1)} %collective-permute-done.kb_ref) | copy-start | bytes 3145732
  34.3 1.5 %copy-start.2 = (bf16[256,2048]{1,0:T(8,128)(2,1)}, bf16[256,2048]{1,0:T(8,128)(2,1)S(1)}, u32[]{:S(2)}) copy-start(bf16[256,2048]{1,0:T(8,128)(2,1)S(1)} %collective-permute-done.1.vb_ref) | copy-start | bytes 3145732

commit v2 on v1

v2 whole, which is shorter than its diff:
```python
import math

import jax
import jax.numpy as jnp
from jax import lax
from jax.experimental import pallas as pl
from jax.experimental.pallas import tpu as pltpu
from jax.sharding import Mesh, PartitionSpec as P

HEADS = 8
MAPS = 16
HD = 128
VD = 256
KEYS = 256
DEVICES = 256
CHIPS = 128
PLANE = 16
COLUMN = 8
SUMS = MAPS * VD
WIDE = SUMS + 128
LINES = 40
NEG = -1e30
AXES = ("x", "z_lo", "y", "z_hi", "core")
BF16 = jnp.bfloat16
F32 = jnp.float32


def attend(place_ref, q_ref, ka_ref, va_ref, kb_ref, vb_ref, out_ref):
    place = place_ref[0]
    core = place % 2
    row = lax.broadcasted_iota(jnp.int32, (CHIPS, 1), 0)
    device = (row // 32) * 64 + ((row // 4) % 2) * 32 + ((row // 8) % 4) * 8 + (row % 4) * 2 + core
    last = device + (DEVICES - 1) * KEYS
    last_a = last - place * KEYS
    last_b = last - (place + 1 - 2 * core) * KEYS
    key = lax.broadcasted_iota(jnp.int32, (CHIPS, KEYS), 1)
    lane = lax.broadcasted_iota(jnp.int32, (CHIPS, 128), 1)
    scaling = math.log2(math.e) / math.sqrt(HD)
    trans = (((1,), (1,)), ((), ()))
    stats = jnp.zeros((CHIPS, 128), F32)
    for index in range(MAPS):
        cols = slice(index * HD, (index + 1) * HD)
        v_cols = slice(index // 2 * VD, (index // 2 + 1) * VD)
        q = q_ref[:, cols]
        sa = lax.dot_general(q, ka_ref[:, cols], trans, preferred_element_type=F32) * scaling
        sb = lax.dot_general(q, kb_ref[:, cols], trans, preferred_element_type=F32) * scaling
        sa = jnp.where(key <= last_a, sa, NEG)
        sb = jnp.where(key <= last_b, sb, NEG)
        top = jnp.max(jnp.maximum(sa, sb), axis=1, keepdims=True).astype(BF16).astype(F32)
        ea = jnp.exp2(sa - top)
        eb = jnp.exp2(sb - top)
        total = jnp.sum(ea + eb, axis=1, keepdims=True)
        acc = jnp.dot(ea.astype(BF16), va_ref[:, v_cols], preferred_element_type=F32)
        acc += jnp.dot(eb.astype(BF16), vb_ref[:, v_cols], preferred_element_type=F32)
        out_ref[:, index * VD : (index + 1) * VD] = acc.astype(BF16)
        high = total.astype(BF16).astype(F32)
        stats = jnp.where(lane == index, top, stats)
        stats = jnp.where(lane == index + MAPS, high, stats)
        stats = jnp.where(lane == index + 2 * MAPS, total - high, stats)
    out_ref[:, SUMS:] = stats.astype(BF16)


def merge_plane(in_ref, out_ref):
    stats = in_ref[:, SUMS:].astype(F32)
    total = pltpu.roll(stats, 128 - MAPS, 1) + pltpu.roll(stats, 128 - 2 * MAPS, 1)
    stats = stats.reshape(PLANE, COLUMN, 128)
    total = total.reshape(PLANE, COLUMN, 128)
    top = jnp.max(stats, axis=0)
    weight = jnp.exp2(stats - top[None])
    total = jnp.sum(weight * total, axis=0)
    lane = lax.broadcasted_iota(jnp.int32, (COLUMN, 128), 1)
    out_ref[pl.ds(2 * MAPS, COLUMN, stride=LINES), :] = jnp.where(
        lane < MAPS, top, pltpu.roll(total, MAPS, 1)
    )
    for line in range(2 * MAPS):
        part = in_ref[:, line * 128 : (line + 1) * 128].astype(F32).reshape(PLANE, COLUMN, 128)
        index = line // 2
        out_ref[pl.ds(line, COLUMN, stride=LINES), :] = jnp.sum(
            part * weight[:, :, index : index + 1], axis=0
        )


def merge_column(lam_ref, in_ref, gain_ref, out_ref):
    stats = in_ref[pl.ds(2 * MAPS, COLUMN, stride=LINES), :]
    total = pltpu.roll(stats, 128 - MAPS, 1)
    top = jnp.max(stats, axis=0, keepdims=True)
    weight = jnp.exp2(stats - top)
    lane = lax.broadcasted_iota(jnp.int32, (COLUMN, 128), 1)
    total = jnp.where(lane < MAPS, jnp.sum(weight * total, axis=0, keepdims=True), 1.0)
    weight = weight / total
    for head in range(HEADS):
        one = weight[:, 2 * head : 2 * head + 1]
        two = weight[:, 2 * head + 1 : 2 * head + 2] * lam_ref[head]
        halves = []
        for half in range(2):
            first = in_ref[pl.ds(4 * head + half, COLUMN, stride=LINES), :] * one
            second = in_ref[pl.ds(4 * head + 2 + half, COLUMN, stride=LINES), :] * two
            halves.append(jnp.sum(first - second, axis=0, keepdims=True))
        diff = jnp.concatenate(halves, axis=1)
        meansq = jnp.mean(diff * diff, axis=1, keepdims=True)
        cols = slice(head * VD, (head + 1) * VD)
        out_ref[:, cols] = (diff / jnp.sqrt(meansq + 1e-5) * gain_ref[:, cols]).astype(BF16)


def shards(queries, key_maps, values, lambdas, norm_gain):
    swap = [(0, 1), (1, 0)]
    key_other = lax.ppermute(key_maps, "core", swap)
    value_other = lax.ppermute(values, "core", swap)
    place = lax.axis_index(AXES).astype(jnp.int32).reshape(1)

    spread = jnp.broadcast_to(queries.reshape(1, MAPS, HD), (COLUMN, MAPS, HD))
    column = lax.all_to_all(spread, ("z_lo", "z_hi"), 0, 0, tiled=True)
    column = column.reshape(1, COLUMN, MAPS * HD)
    spread = jnp.broadcast_to(column, (PLANE, COLUMN, MAPS * HD))
    q_all = lax.all_to_all(spread, ("x", "y"), 0, 0, tiled=True).reshape(CHIPS, MAPS * HD)

    smem = pl.BlockSpec(memory_space=pltpu.SMEM)
    vmem = pl.BlockSpec(memory_space=pltpu.VMEM)
    partial = pl.pallas_call(
        attend,
        in_specs=[smem, vmem, vmem, vmem, vmem, vmem],
        out_specs=vmem,
        out_shape=jax.ShapeDtypeStruct((CHIPS, WIDE), BF16),
        compiler_params=pltpu.CompilerParams(vmem_limit_bytes=16 << 20),
        name="attend",
    )(place, q_all, key_maps, values, key_other, value_other)

    partial = partial.reshape(PLANE, COLUMN, WIDE)
    partial = lax.all_to_all(partial, ("x", "y"), 0, 0, tiled=True)
    merged = pl.pallas_call(
        merge_plane,
        in_specs=[vmem],
        out_specs=vmem,
        out_shape=jax.ShapeDtypeStruct((COLUMN * LINES, 128), F32),
        compiler_params=pltpu.CompilerParams(vmem_limit_bytes=8 << 20),
        name="merge_plane",
    )(partial.reshape(CHIPS, WIDE))
    merged = merged.reshape(COLUMN, LINES, 128)
    merged = lax.all_to_all(merged, ("z_lo", "z_hi"), 0, 0, tiled=True)
    return pl.pallas_call(
        merge_column,
        in_specs=[smem, vmem, vmem],
        out_specs=vmem,
        out_shape=jax.ShapeDtypeStruct((1, HEADS * VD), BF16),
        compiler_params=pltpu.CompilerParams(vmem_limit_bytes=8 << 20),
        name="merge_column",
    )(lambdas, merged.reshape(COLUMN * LINES, 128), norm_gain.reshape(1, HEADS * VD))


def solution(mesh):
    fine = Mesh(mesh.devices.reshape(4, 2, 4, 4, 2), AXES)
    rows = P(AXES, None)
    return jax.shard_map(
        shards,
        mesh=fine,
        in_specs=(rows, rows, rows, P(), P()),
        out_specs=rows,
        check_vma=False,
    )
```

time: 81.6 us -> 71.6 us (0.88)
  Pallas kernels: 12.6 us -> 5.33 us
  local copies, waits for them, and re-layouts: 4.05 us -> 2.11 us
    pallas_call x3, Pallas kernels: 12.6 us -> 5.33 us  [the longest x1 3.52 us: shards(): pl.pallas_call(attend, in_specs=[smem, vmem, vmem, vmem, vmem, vmem], out...]
    all_to_all x1, blocking collectives: 19.7 us -> 18.5 us  [shards(): partial = lax.all_to_all(partial, ('x', 'y'), 0, 0, tiled=True)]
    all_to_all x1 -> x0, local copies, waits for them, and re-layouts: 1.04 us -> none  [shards(): merged = lax.all_to_all(merged, ('z_lo', 'z_hi'), 0, 0, tiled=True)]
    unnamed x8 -> x9, local copies, waits for them, and re-layouts: 2.15 us -> 1.24 us
where the time goes in v2:
time: 71.6 us; the launch traced here: 71.2 us
  blocking collectives  45.1 us (63%)
  waiting for transfers between devices  10.3 us (14%)
  starting transfers between devices  7.54 us (11%)
  Pallas kernels  5.33 us (7%)
  local copies, waits for them, and re-layouts  2.11 us (3%)
  other arithmetic  0.73 us (1%)
    all_to_all x1, blocking collectives, shards(): partial = lax.all_to_all(partial, ('x', 'y'), 0, 0, tiled=True)  18.5 us
    all_to_all x1, blocking collectives, shards(): column = lax.all_to_all(spread, ('z_lo', 'z_hi'), 0, 0, tiled=True)  14.9 us
    all_to_all x1, blocking collectives, shards(): merged = lax.all_to_all(merged, ('z_lo', 'z_hi'), 0, 0, tiled=True)  11.7 us
    all_to_all x1, waiting for transfers between devices, shards(): lax.all_to_all(spread, ('x', 'y'), 0, 0, tiled=True)  10.3 us
    all_to_all x1, starting transfers between devices, shards(): lax.all_to_all(spread, ('x', 'y'), 0, 0, tiled=True)  7.03 us
    pallas_call x1, Pallas kernels, shards(): pl.pallas_call(attend, in_specs=[smem, vmem, vmem, vmem, vmem, vmem], out...  3.52 us
  transfers between devices with their start and end apart: 3, of which 1 were waited for; matrix products, arithmetic and copies ran while one was open for 2% of the time, Pallas kernels for 0%

profile of v2, /device:TPU:32, one launch (start us, length us, event | category | flops | bytes accessed | tf_op | source)
XLA Modules:
  0.0 71.2 jit_solution(6643568068791890313)
XLA Ops:
  0.0 0.0 copy-start
  0.0 0.0 collective-permute-start
  0.0 0.5 collective-permute-start.1
  0.5 0.7 %reduce = bf16[2048]{0:T(1024)(128)(2,1)S(1)} reduce(bf16[1,2048]{1,0:T(2,128)(2,1)} %param.5, bf16[]{:T(256)} %constant.28), dimensions={0}, to_apply=%param.5.reduce_sub_computation | reduce | bytes 8194 | tf_op args[0]
  1.3 14.9 %all_to_all.20 = bf16[8,16,128]{2,1,0:T(8,128)(2,1)S(1)} all-to-all(bf16[8,16,128]{2,1,0:T(8,128)(2,1)S(1)} %broadcast_in_dim.15), channel_id=1, replica_groups=mesh['x'=4,'z_lo'=2,'y'=4,'z_hi'=4,'core'=2] {'z_lo','z_hi'}, dimensions={0} | all-to-all | bytes 65536 | tf_op jit(solution)/shard_map/all_to_all | solution.py:112
  16.2 0.9 %broadcast_in_dim.17 = bf16[16,8,2048]{2,1,0:T(8,128)(2,1)} broadcast(bf16[8,2048]{1,0:T(8,128)(2,1)S(1)} %bitcast.18), dimensions={1,2} | broadcast | bytes 557056 | tf_op jit(solution)/shard_map/broadcast_in_dim | solution.py:114
  17.1 7.0 %all-to-all-start.1 = ((bf16[16,8,2048]{2,1,0:T(8,128)(2,1)}), bf16[16,8,2048]{2,1,0:T(8,128)(2,1)S(1)}, u32[]{:S(2)}, u32[]{:S(2)}) async-start(bf16[16,8,2048]{2,1,0:T(8,128)(2,1)} %broadcast_in_dim.17), calls=%async_computation.1 | async-start | bytes 1048576 | tf_op jit(solution)/shard_map/all_to_all | solution.py:115
  24.1 10.3 %all-to-all-done.1 = bf16[16,8,2048]{2,1,0:T(8,128)(2,1)S(1)} async-done(((bf16[16,8,2048]{2,1,0:T(8,128)(2,1)}), bf16[16,8,2048]{2,1,0:T(8,128)(2,1)S(1)}, u32[]{:S(2)}, u32[]{:S(2)}) %all-to-all-start.1) | async-done | bytes 524320 | tf_op jit(solution)/shard_map/all_to_all | solution.py:115
  34.4 0.0 collective-permute-done.kb_ref
  34.4 0.0 collective-permute-done.1.vb_ref
  34.4 0.0 copy-done
  34.4 0.0 copy-start.1
  34.4 1.2 %copy-done.1 = bf16[256,2048]{1,0:T(8,128)(2,1)S(1)} copy-done((bf16[256,2048]{1,0:T(8,128)(2,1)S(1)}, bf16[256,2048]{1,0:T(8,128)(2,1)}, u32[]{:S(2)}) %copy-start.1) | copy-done | bytes 1048600
  35.7 3.5 %attend.1 = bf16[128,4224]{1,0:T(8,128)(2,1)S(1)} custom-call(s32[1]{0:T(128)} %bitcast.place_ref, bf16[128,2048]{1,0:T(8,128)(2,1)S(1)} %bitcast.14, bf16[256,2048]{1,0:T(8,128)(2,1)S(1)} %copy-done, bf16[256,2048]{1,0:T(8,128)(2,1)S(1)} %copy-done.1, bf16[256,2048]{1,0:T(8,128)(2,1)S(1)} %collective-permute-done.kb_ref, ...), custom_call_target="tpu_custom_call" | custom-call | tf_op jit(solution)/shard_map/attend/pallas_call | solution.py:119
  39.2 18.5 %all_to_all.21 = bf16[16,8,4224]{2,1,0:T(8,128)(2,1)S(1)} all-to-all(bf16[16,8,4224]{2,1,0:T(8,128)(2,1)S(1)} %bitcast.13), channel_id=1, replica_groups=mesh['x'=4,'z_lo'=2,'y'=4,'z_hi'=4,'core'=2] {'x','y'}, dimensions={0} | all-to-all | bytes 2162688 | tf_op jit(solution)/shard_map/all_to_all | solution.py:129
  57.7 0.0 copy-start.2
  57.7 0.0 copy-start.3
  57.7 0.4 merge_plane.1
  58.1 11.7 %all_to_all.22 = f32[8,40,128]{2,1,0:T(8,128)S(1)} all-to-all(f32[8,40,128]{2,1,0:T(8,128)S(1)} %bitcast.15), channel_id=1, replica_groups=mesh['x'=4,'z_lo'=2,'y'=4,'z_hi'=4,'core'=2] {'z_lo','z_hi'}, dimensions={0} | all-to-all | bytes 327680 | tf_op jit(solution)/shard_map/all_to_all | solution.py:139
  69.7 0.0 copy-done.2
  69.7 0.0 copy-done.3
  69.7 1.4 %merge_column.1 = bf16[1,2048]{1,0:T(2,128)(2,1)} custom-call(f32[8]{0:T(128)S(1)} %copy-done.3, f32[320,128]{1,0:T(8,128)S(1)} %bitcast.16, f32[1,2048]{1,0:T(1,128)S(1)} %bitcast.17), custom_call_target="tpu_custom_call" | custom-call | tf_op jit(solution)/shard_map/merge_column/pallas_call | solution.py:140
  (2 shorter events, 0.0 us)
Async XLA Ops:
  0.0 34.4 %copy-start = (bf16[256,2048]{1,0:T(8,128)(2,1)S(1)}, bf16[256,2048]{1,0:T(8,128)(2,1)}, u32[]{:S(2)}) copy-start(bf16[256,2048]{1,0:T(8,128)(2,1)} %ka_ref.1) | copy-start | bytes 3145732
  0.0 34.4 %collective-permute-start = (bf16[256,2048]{1,0:T(8,128)(2,1)}, bf16[256,2048]{1,0:T(8,128)(2,1)S(1)}, u32[]{:S(2)}, u32[]{:S(2)}) collective-permute-start(bf16[256,2048]{1,0:T(8,128)(2,1)} %ka_ref.1), channel_id=1, source_target_pairs={{0,1},{1,0},{2,3},{3,2},{4,5},{5,4},{6,7},{7,6},{8,9},{9,8},{10,11... | collective-permute-start | bytes 3145736 | tf_op jit(solution)/shard_map/ppermute | solution.py:107
  0.0 34.4 %collective-permute-start.1 = (bf16[256,2048]{1,0:T(8,128)(2,1)}, bf16[256,2048]{1,0:T(8,128)(2,1)}, u32[]{:S(2)}, u32[]{:S(2)}) collective-permute-start(bf16[256,2048]{1,0:T(8,128)(2,1)} %va_ref.1), channel_id=1, source_target_pairs={{0,1},{1,0},{2,3},{3,2},{4,5},{5,4},{6,7},{7,6},{8,9},{9,8},{10,11... | collective-permute-start | bytes 3145736 | tf_op jit(solution)/shard_map/ppermute | solution.py:108
  17.1 17.4 %all-to-all-start.1 = ((bf16[16,8,2048]{2,1,0:T(8,128)(2,1)}), bf16[16,8,2048]{2,1,0:T(8,128)(2,1)S(1)}, u32[]{:S(2)}, u32[]{:S(2)}) async-start(bf16[16,8,2048]{2,1,0:T(8,128)(2,1)} %broadcast_in_dim.17), calls=%async_computation.1 | async-start | bytes 1048576 | tf_op jit(solution)/shard_map/all_to_all | solution.py:115
  34.4 1.2 %copy-start.1 = (bf16[256,2048]{1,0:T(8,128)(2,1)S(1)}, bf16[256,2048]{1,0:T(8,128)(2,1)}, u32[]{:S(2)}) copy-start(bf16[256,2048]{1,0:T(8,128)(2,1)} %va_ref.1) | copy-start | bytes 3145732
  57.7 12.0 %copy-start.2 = (f32[2048]{0:T(1024)S(1)}, f32[2048]{0:T(1024)}, u32[]{:S(2)}) copy-start(f32[2048]{0:T(1024)} %param.9) | copy-start | bytes 24580
  57.7 12.0 %copy-start.3 = (f32[8]{0:T(128)S(1)}, f32[8]{0:T(128)}, u32[]{:S(2)}) copy-start(f32[8]{0:T(128)} %lam_ref.1) | copy-start | bytes 100

commit v3 on v2

v3 whole, which is shorter than its diff:
```python
import math

import jax
import jax.numpy as jnp
from jax import lax
from jax.experimental import pallas as pl
from jax.experimental.pallas import tpu as pltpu
from jax.sharding import Mesh, PartitionSpec as P

HEADS = 8
MAPS = 16
HD = 128
VD = 256
KEYS = 256
DEVICES = 256
CHIPS = 128
PLANE = 16
COLUMN = 8
SUMS = MAPS * VD
WIDE = SUMS + 128
LINES = 40
LAG = 4
NEG = -1e30
AXES = ("x", "z_lo", "y", "z_hi", "core")
BF16 = jnp.bfloat16
F32 = jnp.float32


def repeat_rows(in_ref, out_ref):
    rows = in_ref[...].astype(F32)
    rows = jnp.concatenate([rows, rows], axis=0).astype(BF16)
    for start in range(0, CHIPS, 2 * COLUMN):
        out_ref[start : start + 2 * COLUMN, :] = rows


def attend(q_ref, ka_ref, kb_ref, va_ref, vb_ref, out_ref):
    core = lax.axis_index("core")
    place = (
        lax.axis_index("x") * 64
        + lax.axis_index("z_lo") * 32
        + lax.axis_index("y") * 8
        + lax.axis_index("z_hi") * 2
        + core
    )
    row = lax.broadcasted_iota(jnp.int32, (CHIPS, 1), 0)
    device = (row // 32) * 64 + ((row // 4) % 2) * 32 + ((row // 8) % 4) * 8 + (row % 4) * 2 + core
    last = device + (DEVICES - 1) * KEYS
    last_a = last - place * KEYS
    last_b = last - (place + 1 - 2 * core) * KEYS
    key = lax.broadcasted_iota(jnp.int32, (CHIPS, KEYS), 1)
    lane = lax.broadcasted_iota(jnp.int32, (CHIPS, 128), 1)
    scaling = math.log2(math.e) / math.sqrt(HD)
    trans = (((1,), (1,)), ((), ()))
    stats = jnp.zeros((CHIPS, 128), F32)
    waiting = []
    for index in range(MAPS + LAG):
        if index < MAPS:
            cols = slice(index * HD, (index + 1) * HD)
            q = q_ref[:, cols]
            sa = lax.dot_general(q, ka_ref[:, cols], trans, preferred_element_type=F32) * scaling
            sb = lax.dot_general(q, kb_ref[:, cols], trans, preferred_element_type=F32) * scaling
            sa = jnp.where(key <= last_a, sa, NEG)
            sb = jnp.where(key <= last_b, sb, NEG)
            top = jnp.max(jnp.maximum(sa, sb), axis=1, keepdims=True).astype(BF16).astype(F32)
            ea = jnp.exp2(sa - top)
            eb = jnp.exp2(sb - top)
            total = jnp.sum(ea + eb, axis=1, keepdims=True)
            waiting.append((ea.astype(BF16), eb.astype(BF16)))
            high = total.astype(BF16).astype(F32)
            stats = jnp.where(lane == index, top, stats)
            stats = jnp.where(lane == index + MAPS, high, stats)
            stats = jnp.where(lane == index + 2 * MAPS, total - high, stats)
        if index >= LAG:
            done = index - LAG
            cols = slice(done // 2 * VD, (done // 2 + 1) * VD)
            ea, eb = waiting[done]
            acc = jnp.dot(ea, va_ref[:, cols], preferred_element_type=F32)
            acc += jnp.dot(eb, vb_ref[:, cols], preferred_element_type=F32)
            out_ref[:, done * VD : (done + 1) * VD] = acc.astype(BF16)
    out_ref[:, SUMS:] = stats.astype(BF16)


def merge_plane(in_ref, out_ref, lines_ref):
    stats = in_ref[:, SUMS:].astype(F32)
    total = pltpu.roll(stats, 128 - MAPS, 1) + pltpu.roll(stats, 128 - 2 * MAPS, 1)
    stats = stats.reshape(PLANE, COLUMN, 128)
    total = total.reshape(PLANE, COLUMN, 128)
    top = jnp.max(stats, axis=0)
    weight = jnp.exp2(stats - top[None])
    total = jnp.sum(weight * total, axis=0)
    lane = lax.broadcasted_iota(jnp.int32, (COLUMN, 128), 1)
    high = total.astype(BF16).astype(F32)
    low = jnp.where(lane < 3 * MAPS, pltpu.roll(total - high, 2 * MAPS, 1), 0.0)
    tail = jnp.where(lane < 2 * MAPS, pltpu.roll(high, MAPS, 1), low)
    lines_ref[pl.ds(2 * MAPS, COLUMN, stride=LINES), :] = jnp.where(lane < MAPS, top, tail)
    for line in range(2 * MAPS + 1, LINES):
        lines_ref[pl.ds(line, COLUMN, stride=LINES), :] = jnp.zeros((COLUMN, 128), F32)
    for line in range(2 * MAPS):
        part = in_ref[:, line * 128 : (line + 1) * 128].astype(F32).reshape(PLANE, COLUMN, 128)
        index = line // 2
        lines_ref[pl.ds(line, COLUMN, stride=LINES), :] = jnp.sum(
            part * weight[:, :, index : index + 1], axis=0
        )
    out_ref[...] = lines_ref[...].astype(BF16)


def merge_column(lam_ref, in_ref, gain_ref, out_ref, lines_ref):
    lines_ref[...] = in_ref[...].astype(F32)
    stats = lines_ref[pl.ds(2 * MAPS, COLUMN, stride=LINES), :]
    total = pltpu.roll(stats, 128 - MAPS, 1) + pltpu.roll(stats, 128 - 2 * MAPS, 1)
    top = jnp.max(stats, axis=0, keepdims=True)
    weight = jnp.exp2(stats - top)
    lane = lax.broadcasted_iota(jnp.int32, (COLUMN, 128), 1)
    total = jnp.where(lane < MAPS, jnp.sum(weight * total, axis=0, keepdims=True), 1.0)
    weight = weight / total
    for head in range(HEADS):
        one = weight[:, 2 * head : 2 * head + 1]
        two = weight[:, 2 * head + 1 : 2 * head + 2] * lam_ref[:, head : head + 1]
        halves = []
        for half in range(2):
            first = lines_ref[pl.ds(4 * head + half, COLUMN, stride=LINES), :] * one
            second = lines_ref[pl.ds(4 * head + 2 + half, COLUMN, stride=LINES), :] * two
            halves.append(jnp.sum(first - second, axis=0, keepdims=True))
        squares = halves[0] * halves[0] + halves[1] * halves[1]
        meansq = jnp.sum(squares, axis=1, keepdims=True) / VD
        factor = 1.0 / jnp.sqrt(meansq + 1e-5)
        for half in range(2):
            cols = slice(head * VD + half * 128, head * VD + half * 128 + 128)
            out_ref[:, cols] = (halves[half] * factor * gain_ref[:, cols]).astype(BF16)


def shards(queries, key_maps, values, lambdas, norm_gain):
    swap = [(0, 1), (1, 0)]
    key_other = lax.ppermute(key_maps, "core", swap)
    value_other = lax.ppermute(values, "core", swap)

    spread = jnp.broadcast_to(queries.reshape(1, MAPS, HD), (COLUMN, MAPS, HD))
    column = lax.all_to_all(spread, ("z_lo", "z_hi"), 0, 0, tiled=True)
    column = column.reshape(COLUMN, MAPS * HD)
    vmem = pl.BlockSpec(memory_space=pltpu.VMEM)
    spread = pl.pallas_call(
        repeat_rows,
        in_specs=[vmem],
        out_specs=vmem,
        out_shape=jax.ShapeDtypeStruct((CHIPS, MAPS * HD), BF16),
        compiler_params=pltpu.CompilerParams(vmem_limit_bytes=8 << 20),
        cost_estimate=pl.CostEstimate(flops=1 << 31, bytes_accessed=1 << 20, transcendentals=0),
        name="repeat_rows",
    )(column)
    spread = spread.reshape(PLANE, COLUMN, MAPS * HD)
    q_all = lax.all_to_all(spread, ("x", "y"), 0, 0, tiled=True).reshape(CHIPS, MAPS * HD)

    partial = pl.pallas_call(
        attend,
        in_specs=[vmem] * 5,
        out_specs=vmem,
        out_shape=jax.ShapeDtypeStruct((CHIPS, WIDE), BF16),
        compiler_params=pltpu.CompilerParams(vmem_limit_bytes=16 << 20),
        name="attend",
    )(q_all, key_maps, key_other, values, value_other)

    partial = partial.reshape(PLANE, COLUMN, WIDE)
    partial = lax.all_to_all(partial, ("x", "y"), 0, 0, tiled=True)
    merged = pl.pallas_call(
        merge_plane,
        in_specs=[vmem],
        out_specs=vmem,
        out_shape=jax.ShapeDtypeStruct((COLUMN * LINES, 128), BF16),
        scratch_shapes=[pltpu.VMEM((COLUMN * LINES, 128), F32)],
        compiler_params=pltpu.CompilerParams(vmem_limit_bytes=8 << 20),
        name="merge_plane",
    )(partial.reshape(CHIPS, WIDE))
    merged = merged.reshape(COLUMN, LINES, 128)
    merged = lax.all_to_all(merged, ("z_lo", "z_hi"), 0, 0, tiled=True)
    return pl.pallas_call(
        merge_column,
        in_specs=[vmem, vmem, vmem],
        out_specs=vmem,
        out_shape=jax.ShapeDtypeStruct((1, HEADS * VD), BF16),
        scratch_shapes=[pltpu.VMEM((COLUMN * LINES, 128), F32)],
        compiler_params=pltpu.CompilerParams(vmem_limit_bytes=8 << 20),
        name="merge_column",
    )(lambdas.reshape(1, HEADS), merged.reshape(COLUMN * LINES, 128), norm_gain.reshape(1, HEADS * VD))


def solution(mesh):
    fine = Mesh(mesh.devices.reshape(4, 2, 4, 4, 2), AXES)
    rows = P(AXES, None)
    return jax.shard_map(
        shards,
        mesh=fine,
        in_specs=(rows, rows, rows, P(), P()),
        out_specs=rows,
        check_vma=False,
    )
```

time: 71.6 us -> 66.3 us (0.926)
  blocking collectives: 45.1 us -> 61.3 us
  waiting for transfers between devices: 10.3 us -> 0.01 us
  starting transfers between devices: 7.54 us -> 0.51 us
  local copies, waits for them, and re-layouts: 2.11 us -> 0.04 us
  Pallas kernels: 5.33 us -> 3.36 us
    all_to_all x0 -> x1, blocking collectives: none -> 17.2 us  [shards(): lax.all_to_all(spread, ('x', 'y'), 0, 0, tiled=True)]
    all_to_all x1 -> x0, waiting for transfers between devices: 10.3 us -> none  [shards(): lax.all_to_all(spread, ('x', 'y'), 0, 0, tiled=True)]
    all_to_all x1 -> x0, starting transfers between devices: 7.03 us -> none  [shards(): lax.all_to_all(spread, ('x', 'y'), 0, 0, tiled=True)]
    pallas_call x2 -> x3, Pallas kernels: 4.95 us -> 2.95 us  [the longest x1 2.01 us: shards(): pl.pallas_call(attend, in_specs=[vmem] * 5, out_specs=vmem, out_shape=jax...]
    unnamed x9, local copies, waits for them, and re-layouts: 1.24 us -> 0.03 us
    all_to_all x1, blocking collectives: 11.7 us -> 10.8 us  [shards(): merged = lax.all_to_all(merged, ('z_lo', 'z_hi'), 0, 0, tiled=True)]
    broadcast_in_dim x1 -> x0, local copies, waits for them, and re-layouts: 0.86 us -> none  [shards(): spread = jnp.broadcast_to(column, (PLANE, COLUMN, MAPS * HD))]
  transfers between devices with their start and end apart: 3 -> 2, of which waited for: 1 -> 0; matrix products, arithmetic and copies ran while one was open for 2% -> 1% of each run, Pallas kernels for 0% -> 0%
where the time goes in v3:
time: 66.3 us; the launch traced here: 66 us
  blocking collectives  61.3 us (92%)
  Pallas kernels  3.36 us (5%)
  other arithmetic  0.73 us (1%)
    all_to_all x1, blocking collectives, shards(): partial = lax.all_to_all(partial, ('x', 'y'), 0, 0, tiled=True)  18.4 us
    all_to_all x1, blocking collectives, shards(): lax.all_to_all(spread, ('x', 'y'), 0, 0, tiled=True)  17.2 us
    all_to_all x1, blocking collectives, shards(): column = lax.all_to_all(spread, ('z_lo', 'z_hi'), 0, 0, tiled=True)  14.9 us
    all_to_all x1, blocking collectives, shards(): merged = lax.all_to_all(merged, ('z_lo', 'z_hi'), 0, 0, tiled=True)  10.8 us
    pallas_call x1, Pallas kernels, shards(): pl.pallas_call(attend, in_specs=[vmem] * 5, out_specs=vmem, out_shape=jax...  2.01 us
  transfers between devices with their start and end apart: 2, of which 0 were waited for; matrix products, arithmetic and copies ran while one was open for 1% of the time, Pallas kernels for 0%

profile of v3, /device:TPU:32, one launch (start us, length us, event | category | flops | bytes accessed | tf_op | source)
XLA Modules:
  0.0 66.0 jit_solution(4710636352166422792)
XLA Ops:
  0.0 0.0 collective-permute-start
  0.0 0.5 collective-permute-start.1
  0.5 0.7 %reduce = bf16[2048]{0:T(1024)(128)(2,1)S(1)} reduce(bf16[1,2048]{1,0:T(2,128)(2,1)} %param.5, bf16[]{:T(256)} %constant.1), dimensions={0}, to_apply=%param.5.reduce_sub_computation | reduce | bytes 8194 | tf_op args[0]
  1.3 14.9 %all_to_all.20 = bf16[8,16,128]{2,1,0:T(8,128)(2,1)S(1)} all-to-all(bf16[8,16,128]{2,1,0:T(8,128)(2,1)S(1)} %broadcast_in_dim.8), channel_id=1, replica_groups=mesh['x'=4,'z_lo'=2,'y'=4,'z_hi'=4,'core'=2] {'z_lo','z_hi'}, dimensions={0} | all-to-all | bytes 65536 | tf_op jit(solution)/shard_map/all_to_all | solution.py:138
  16.2 0.0 copy-start.1
  16.3 0.0 copy-start
  16.3 17.2 %all_to_all.21 = bf16[16,8,2048]{2,1,0:T(8,128)(2,1)S(1)} all-to-all(bf16[16,8,2048]{2,1,0:T(8,128)(2,1)S(1)} %bitcast.16), channel_id=1, replica_groups=mesh['x'=4,'z_lo'=2,'y'=4,'z_hi'=4,'core'=2] {'x','y'}, dimensions={0} | all-to-all | bytes 1048576 | tf_op jit(solution)/shard_map/all_to_all | solution.py:151
  33.5 0.0 collective-permute-done.kb_ref
  33.5 0.0 collective-permute-done.1.vb_ref
  33.5 0.0 copy-done.1
  33.5 0.0 copy-done
  33.5 2.0 %attend.1 = bf16[128,4224]{1,0:T(8,128)(2,1)S(1)} custom-call(bf16[128,2048]{1,0:T(8,128)(2,1)S(1)} %bitcast.15, bf16[256,2048]{1,0:T(8,128)(2,1)S(1)} %copy-done, bf16[256,2048]{1,0:T(8,128)(2,1)S(1)} %collective-permute-done.kb_ref, bf16[256,2048]{1,0:T(8,128)(2,1)S(1)} %copy-done.1, bf16[256,2048]{1,0:T(8,128)(2,1)S(1)} %collective-permute-done.1.vb_ref), custom_call_target="tpu_custom_call" | custom-call | tf_op jit(solution)/shard_map/attend/pallas_call | solution.py:153
  35.5 18.4 %all_to_all.22 = bf16[16,8,4224]{2,1,0:T(8,128)(2,1)S(1)} all-to-all(bf16[16,8,4224]{2,1,0:T(8,128)(2,1)S(1)} %bitcast.14), channel_id=1, replica_groups=mesh['x'=4,'z_lo'=2,'y'=4,'z_hi'=4,'core'=2] {'x','y'}, dimensions={0} | all-to-all | bytes 2162688 | tf_op jit(solution)/shard_map/all_to_all | solution.py:163
  53.9 0.0 copy-start.2
  53.9 0.0 copy-start.3
  53.9 0.4 merge_plane.1
  54.3 10.8 %all_to_all.23 = bf16[8,40,128]{2,1,0:T(8,128)(2,1)S(1)} all-to-all(bf16[8,40,128]{2,1,0:T(8,128)(2,1)S(1)} %bitcast.17), channel_id=1, replica_groups=mesh['x'=4,'z_lo'=2,'y'=4,'z_hi'=4,'core'=2] {'z_lo','z_hi'}, dimensions={0} | all-to-all | bytes 163840 | tf_op jit(solution)/shard_map/all_to_all | solution.py:174
  65.1 0.0 copy-done.2
  65.1 0.0 copy-done.3
  65.1 0.9 %merge_column.1 = bf16[1,2048]{1,0:T(2,128)(2,1)} custom-call(f32[1,8]{1,0:T(1,128)S(1)} %bitcast.21, bf16[320,128]{1,0:T(8,128)(2,1)S(1)} %bitcast.18, f32[1,2048]{1,0:T(1,128)S(1)} %bitcast.20), custom_call_target="tpu_custom_call" | custom-call | tf_op jit(solution)/shard_map/merge_column/pallas_call | solution.py:175
  (3 shorter events, 0.1 us)
Async XLA Ops:
  0.0 33.5 %collective-permute-start = (bf16[256,2048]{1,0:T(8,128)(2,1)}, bf16[256,2048]{1,0:T(8,128)(2,1)S(1)}, u32[]{:S(2)}, u32[]{:S(2)}) collective-permute-start(bf16[256,2048]{1,0:T(8,128)(2,1)} %ka_ref.1), channel_id=1, source_target_pairs={{0,1},{1,0},{2,3},{3,2},{4,5},{5,4},{6,7},{7,6},{8,9},{9,8},{10,11... | collective-permute-start | bytes 3145736 | tf_op jit(solution)/shard_map/ppermute | solution.py:134
  0.0 33.5 %collective-permute-start.1 = (bf16[256,2048]{1,0:T(8,128)(2,1)}, bf16[256,2048]{1,0:T(8,128)(2,1)S(1)}, u32[]{:S(2)}, u32[]{:S(2)}) collective-permute-start(bf16[256,2048]{1,0:T(8,128)(2,1)} %va_ref.1), channel_id=1, source_target_pairs={{0,1},{1,0},{2,3},{3,2},{4,5},{5,4},{6,7},{7,6},{8,9},{9,8},{10,11... | collective-permute-start | bytes 3145736 | tf_op jit(solution)/shard_map/ppermute | solution.py:135
  16.2 17.3 %copy-start.1 = (bf16[256,2048]{1,0:T(8,128)(2,1)S(1)}, bf16[256,2048]{1,0:T(8,128)(2,1)}, u32[]{:S(2)}) copy-start(bf16[256,2048]{1,0:T(8,128)(2,1)} %va_ref.1) | copy-start | bytes 3145732
  16.3 17.2 %copy-start = (bf16[256,2048]{1,0:T(8,128)(2,1)S(1)}, bf16[256,2048]{1,0:T(8,128)(2,1)}, u32[]{:S(2)}) copy-start(bf16[256,2048]{1,0:T(8,128)(2,1)} %ka_ref.1) | copy-start | bytes 3145732
  53.9 11.2 %copy-start.2 = (f32[2048]{0:T(1024)S(1)}, f32[2048]{0:T(1024)}, u32[]{:S(2)}) copy-start(f32[2048]{0:T(1024)} %param.9) | copy-start | bytes 24580
  53.9 11.2 %copy-start.3 = (f32[8]{0:T(128)S(1)}, f32[8]{0:T(128)}, u32[]{:S(2)}) copy-start(f32[8]{0:T(128)} %param.8) | copy-start | bytes 100

commit v4 on v3

--- a/solution.py
+++ b/solution.py
@@ -19,7 +19,7 @@
 SUMS = MAPS * VD
 WIDE = SUMS + 128
 LINES = 40
-LAG = 4
+LAG = 3
 NEG = -1e30
 AXES = ("x", "z_lo", "y", "z_hi", "core")
 BF16 = jnp.bfloat16
@@ -33,7 +33,7 @@
         out_ref[start : start + 2 * COLUMN, :] = rows
 
 
-def attend(q_ref, ka_ref, kb_ref, va_ref, vb_ref, out_ref):
+def attend(q_ref, ka_ref, kb_ref, va_ref, vb_ref, out_ref, mask_ref):
     core = lax.axis_index("core")
     place = (
         lax.axis_index("x") * 64
@@ -48,6 +48,8 @@
     last_a = last - place * KEYS
     last_b = last - (place + 1 - 2 * core) * KEYS
     key = lax.broadcasted_iota(jnp.int32, (CHIPS, KEYS), 1)
+    mask_ref[:, :KEYS] = jnp.where(key <= last_a, 0.0, NEG)
+    mask_ref[:, KEYS:] = jnp.where(key <= last_b, 0.0, NEG)
     lane = lax.broadcasted_iota(jnp.int32, (CHIPS, 128), 1)
     scaling = math.log2(math.e) / math.sqrt(HD)
     trans = (((1,), (1,)), ((), ()))
@@ -59,17 +61,15 @@
             q = q_ref[:, cols]
             sa = lax.dot_general(q, ka_ref[:, cols], trans, preferred_element_type=F32) * scaling
             sb = lax.dot_general(q, kb_ref[:, cols], trans, preferred_element_type=F32) * scaling
-            sa = jnp.where(key <= last_a, sa, NEG)
-            sb = jnp.where(key <= last_b, sb, NEG)
+            sa = sa + mask_ref[:, :KEYS]
+            sb = sb + mask_ref[:, KEYS:]
             top = jnp.max(jnp.maximum(sa, sb), axis=1, keepdims=True).astype(BF16).astype(F32)
             ea = jnp.exp2(sa - top)
             eb = jnp.exp2(sb - top)
             total = jnp.sum(ea + eb, axis=1, keepdims=True)
             waiting.append((ea.astype(BF16), eb.astype(BF16)))
-            high = total.astype(BF16).astype(F32)
             stats = jnp.where(lane == index, top, stats)
-            stats = jnp.where(lane == index + MAPS, high, stats)
-            stats = jnp.where(lane == index + 2 * MAPS, total - high, stats)
+            stats = jnp.where(lane == index + MAPS, total, stats)
         if index >= LAG:
             done = index - LAG
             cols = slice(done // 2 * VD, (done // 2 + 1) * VD)
@@ -77,7 +77,9 @@
             acc = jnp.dot(ea, va_ref[:, cols], preferred_element_type=F32)
             acc += jnp.dot(eb, vb_ref[:, cols], preferred_element_type=F32)
             out_ref[:, done * VD : (done + 1) * VD] = acc.astype(BF16)
-    out_ref[:, SUMS:] = stats.astype(BF16)
+    high = stats.astype(BF16).astype(F32)
+    low = jnp.where(lane < 3 * MAPS, pltpu.roll(stats - high, MAPS, 1), 0.0)
+    out_ref[:, SUMS:] = jnp.where(lane < 2 * MAPS, high, low).astype(BF16)
 
 
 def merge_plane(in_ref, out_ref, lines_ref):
@@ -144,7 +146,7 @@
         out_specs=vmem,
         out_shape=jax.ShapeDtypeStruct((CHIPS, MAPS * HD), BF16),
         compiler_params=pltpu.CompilerParams(vmem_limit_bytes=8 << 20),
-        cost_estimate=pl.CostEstimate(flops=1 << 31, bytes_accessed=1 << 20, transcendentals=0),
+        cost_estimate=pl.CostEstimate(flops=1 << 34, bytes_accessed=1 << 20, transcendentals=0),
         name="repeat_rows",
     )(column)
     spread = spread.reshape(PLANE, COLUMN, MAPS * HD)
@@ -155,6 +157,7 @@
         in_specs=[vmem] * 5,
         out_specs=vmem,
         out_shape=jax.ShapeDtypeStruct((CHIPS, WIDE), BF16),
+        scratch_shapes=[pltpu.VMEM((CHIPS, 2 * KEYS), F32)],
         compiler_params=pltpu.CompilerParams(vmem_limit_bytes=16 << 20),
         name="attend",
     )(q_all, key_maps, key_other, values, value_other)

time: 66.3 us -> 66.1 us (level)
  blocking collectives: 61.3 us -> 46 us
  starting transfers between devices: 0.51 us -> 9.08 us
  waiting for transfers between devices: 0.01 us -> 6.06 us
    all_to_all x1 -> x0, blocking collectives: 14.9 us -> none  [shards(): column = lax.all_to_all(spread, ('z_lo', 'z_hi'), 0, 0, tiled=True)]
    all_to_all x0 -> x1, starting transfers between devices: none -> 8.57 us  [shards(): column = lax.all_to_all(spread, ('z_lo', 'z_hi'), 0, 0, tiled=True)]
    all_to_all x0 -> x1, waiting for transfers between devices: none -> 6.05 us  [shards(): column = lax.all_to_all(spread, ('z_lo', 'z_hi'), 0, 0, tiled=True)]
  transfers between devices with their start and end apart: 2 -> 3, of which waited for: 0 -> 1; matrix products, arithmetic and copies ran while one was open for 1% -> 0% of each run, Pallas kernels for 0% -> 0%
where the time goes in v4:
time: 66.1 us; the launch traced here: 65.8 us
  blocking collectives  46 us (70%)
  starting transfers between devices  9.08 us (14%)
  waiting for transfers between devices  6.06 us (9%)
  Pallas kernels  3.21 us (5%)
  other arithmetic  0.73 us (1%)
    all_to_all x1, blocking collectives, shards(): partial = lax.all_to_all(partial, ('x', 'y'), 0, 0, tiled=True)  18.3 us
    all_to_all x1, blocking collectives, shards(): lax.all_to_all(spread, ('x', 'y'), 0, 0, tiled=True)  17.1 us
    all_to_all x1, blocking collectives, shards(): merged = lax.all_to_all(merged, ('z_lo', 'z_hi'), 0, 0, tiled=True)  10.7 us
    all_to_all x1, starting transfers between devices, shards(): column = lax.all_to_all(spread, ('z_lo', 'z_hi'), 0, 0, tiled=True)  8.57 us
    all_to_all x1, waiting for transfers between devices, shards(): column = lax.all_to_all(spread, ('z_lo', 'z_hi'), 0, 0, tiled=True)  6.05 us
    pallas_call x1, Pallas kernels, shards(): pl.pallas_call(attend, in_specs=[vmem] * 5, out_specs=vmem, out_shape=jax...  1.85 us
  transfers between devices with their start and end apart: 3, of which 1 were waited for; matrix products, arithmetic and copies ran while one was open for 0% of the time, Pallas kernels for 0%

profile of v4, /device:TPU:32, one launch (start us, length us, event | category | flops | bytes accessed | tf_op | source)
XLA Modules:
  0.0 65.8 jit_solution(12244460345603884884)
XLA Ops:
  0.0 0.7 %reduce = bf16[2048]{0:T(1024)(128)(2,1)S(1)} reduce(bf16[1,2048]{1,0:T(2,128)(2,1)} %param.5, bf16[]{:T(256)} %constant.1), dimensions={0}, to_apply=%param.5.reduce_sub_computation | reduce | bytes 8194 | tf_op args[0]
  0.7 0.6 broadcast_in_dim.8
  1.3 8.6 %all-to-all-start = ((bf16[8,16,128]{2,1,0:T(8,128)(2,1)}), bf16[8,16,128]{2,1,0:T(8,128)(2,1)S(1)}, u32[]{:S(2)}, u32[]{:S(2)}) async-start(bf16[8,16,128]{2,1,0:T(8,128)(2,1)} %broadcast_in_dim.8), calls=%async_computation | async-start | bytes 65536 | tf_op jit(solution)/shard_map/all_to_all | solution.py:140
  9.9 0.0 collective-permute-start
  9.9 0.5 collective-permute-start.1
  10.4 6.1 %all-to-all-done = bf16[8,16,128]{2,1,0:T(8,128)(2,1)S(1)} async-done(((bf16[8,16,128]{2,1,0:T(8,128)(2,1)}), bf16[8,16,128]{2,1,0:T(8,128)(2,1)S(1)}, u32[]{:S(2)}, u32[]{:S(2)}) %all-to-all-start) | async-done | bytes 32800 | tf_op jit(solution)/shard_map/all_to_all | solution.py:140
  16.5 0.0 copy-start.1
  16.6 0.0 copy-start
  16.6 17.1 %all_to_all.20 = bf16[16,8,2048]{2,1,0:T(8,128)(2,1)S(1)} all-to-all(bf16[16,8,2048]{2,1,0:T(8,128)(2,1)S(1)} %bitcast.16), channel_id=1, replica_groups=mesh['x'=4,'z_lo'=2,'y'=4,'z_hi'=4,'core'=2] {'x','y'}, dimensions={0} | all-to-all | bytes 1048576 | tf_op jit(solution)/shard_map/all_to_all | solution.py:153
  33.6 0.0 collective-permute-done.kb_ref
  33.6 0.0 collective-permute-done.1.vb_ref
  33.6 0.0 copy-done.1
  33.6 0.0 copy-done
  33.7 1.9 %attend.1 = bf16[128,4224]{1,0:T(8,128)(2,1)S(1)} custom-call(bf16[128,2048]{1,0:T(8,128)(2,1)S(1)} %bitcast.15, bf16[256,2048]{1,0:T(8,128)(2,1)S(1)} %copy-done, bf16[256,2048]{1,0:T(8,128)(2,1)S(1)} %collective-permute-done.kb_ref, bf16[256,2048]{1,0:T(8,128)(2,1)S(1)} %copy-done.1, bf16[256,2048]{1,0:T(8,128)(2,1)S(1)} %collective-permute-done.1.vb_ref), custom_call_target="tpu_custom_call" | custom-call | tf_op jit(solution)/shard_map/attend/pallas_call | solution.py:155
  35.5 18.3 %all_to_all.21 = bf16[16,8,4224]{2,1,0:T(8,128)(2,1)S(1)} all-to-all(bf16[16,8,4224]{2,1,0:T(8,128)(2,1)S(1)} %bitcast.14), channel_id=1, replica_groups=mesh['x'=4,'z_lo'=2,'y'=4,'z_hi'=4,'core'=2] {'x','y'}, dimensions={0} | all-to-all | bytes 2162688 | tf_op jit(solution)/shard_map/all_to_all | solution.py:166
  53.8 0.0 copy-start.2
  53.8 0.0 copy-start.3
  53.8 0.4 merge_plane.1
  54.2 10.7 %all_to_all.22 = bf16[8,40,128]{2,1,0:T(8,128)(2,1)S(1)} all-to-all(bf16[8,40,128]{2,1,0:T(8,128)(2,1)S(1)} %bitcast.17), channel_id=1, replica_groups=mesh['x'=4,'z_lo'=2,'y'=4,'z_hi'=4,'core'=2] {'z_lo','z_hi'}, dimensions={0} | all-to-all | bytes 163840 | tf_op jit(solution)/shard_map/all_to_all | solution.py:177
  64.9 0.0 copy-done.2
  64.9 0.0 copy-done.3
  64.9 0.9 %merge_column.1 = bf16[1,2048]{1,0:T(2,128)(2,1)} custom-call(f32[1,8]{1,0:T(1,128)S(1)} %bitcast.21, bf16[320,128]{1,0:T(8,128)(2,1)S(1)} %bitcast.18, f32[1,2048]{1,0:T(1,128)S(1)} %bitcast.20), custom_call_target="tpu_custom_call" | custom-call | tf_op jit(solution)/shard_map/merge_column/pallas_call | solution.py:178
  (2 shorter events, 0.1 us)
Async XLA Ops:
  1.3 15.1 %all-to-all-start = ((bf16[8,16,128]{2,1,0:T(8,128)(2,1)}), bf16[8,16,128]{2,1,0:T(8,128)(2,1)S(1)}, u32[]{:S(2)}, u32[]{:S(2)}) async-start(bf16[8,16,128]{2,1,0:T(8,128)(2,1)} %broadcast_in_dim.8), calls=%async_computation | async-start | bytes 65536 | tf_op jit(solution)/shard_map/all_to_all | solution.py:140
  9.9 23.7 %collective-permute-start = (bf16[256,2048]{1,0:T(8,128)(2,1)}, bf16[256,2048]{1,0:T(8,128)(2,1)S(1)}, u32[]{:S(2)}, u32[]{:S(2)}) collective-permute-start(bf16[256,2048]{1,0:T(8,128)(2,1)} %ka_ref.1), channel_id=1, source_target_pairs={{0,1},{1,0},{2,3},{3,2},{4,5},{5,4},{6,7},{7,6},{8,9},{9,8},{10,11... | collective-permute-start | bytes 3145736 | tf_op jit(solution)/shard_map/ppermute | solution.py:136
  9.9 23.7 %collective-permute-start.1 = (bf16[256,2048]{1,0:T(8,128)(2,1)}, bf16[256,2048]{1,0:T(8,128)(2,1)S(1)}, u32[]{:S(2)}, u32[]{:S(2)}) collective-permute-start(bf16[256,2048]{1,0:T(8,128)(2,1)} %va_ref.1), channel_id=1, source_target_pairs={{0,1},{1,0},{2,3},{3,2},{4,5},{5,4},{6,7},{7,6},{8,9},{9,8},{10,11... | collective-permute-start | bytes 3145736 | tf_op jit(solution)/shard_map/ppermute | solution.py:137
  16.5 17.1 %copy-start.1 = (bf16[256,2048]{1,0:T(8,128)(2,1)S(1)}, bf16[256,2048]{1,0:T(8,128)(2,1)}, u32[]{:S(2)}) copy-start(bf16[256,2048]{1,0:T(8,128)(2,1)} %va_ref.1) | copy-start | bytes 3145732
  16.6 17.1 %copy-start = (bf16[256,2048]{1,0:T(8,128)(2,1)S(1)}, bf16[256,2048]{1,0:T(8,128)(2,1)}, u32[]{:S(2)}) copy-start(bf16[256,2048]{1,0:T(8,128)(2,1)} %ka_ref.1) | copy-start | bytes 3145732
  53.8 11.1 %copy-start.2 = (f32[2048]{0:T(1024)S(1)}, f32[2048]{0:T(1024)}, u32[]{:S(2)}) copy-start(f32[2048]{0:T(1024)} %param.9) | copy-start | bytes 24580
  53.8 11.1 %copy-start.3 = (f32[8]{0:T(128)S(1)}, f32[8]{0:T(128)}, u32[]{:S(2)}) copy-start(f32[8]{0:T(128)} %param.8) | copy-start | bytes 100

commit v5 on v4

--- a/solution.py
+++ b/solution.py
@@ -26,14 +26,7 @@
 F32 = jnp.float32
 
 
-def repeat_rows(in_ref, out_ref):
-    rows = in_ref[...].astype(F32)
-    rows = jnp.concatenate([rows, rows], axis=0).astype(BF16)
-    for start in range(0, CHIPS, 2 * COLUMN):
-        out_ref[start : start + 2 * COLUMN, :] = rows
-
-
-def attend(q_ref, ka_ref, kb_ref, va_ref, vb_ref, out_ref, mask_ref):
+def causal_mask(mask_ref):
     core = lax.axis_index("core")
     place = (
         lax.axis_index("x") * 64
@@ -50,6 +43,24 @@
     key = lax.broadcasted_iota(jnp.int32, (CHIPS, KEYS), 1)
     mask_ref[:, :KEYS] = jnp.where(key <= last_a, 0.0, NEG)
     mask_ref[:, KEYS:] = jnp.where(key <= last_b, 0.0, NEG)
+
+
+def own_row(in_ref, mask_ref, out_ref):
+    row = in_ref[...].astype(F32)
+    tall = jnp.concatenate([row[:, start * HD : (start + 1) * HD] for start in range(MAPS)], axis=0)
+    tall = tall.astype(BF16)
+    for copy in range(COLUMN):
+        out_ref[copy] = tall
+
+
+def repeat_rows(in_ref, out_ref):
+    rows = in_ref[...].astype(F32)
+    rows = jnp.concatenate([rows, rows], axis=0).astype(BF16)
+    for start in range(0, CHIPS, 2 * COLUMN):
+        out_ref[start : start + 2 * COLUMN, :] = rows
+
+
+def attend(q_ref, ka_ref, kb_ref, va_ref, vb_ref, mask_ref, out_ref):
     lane = lax.broadcasted_iota(jnp.int32, (CHIPS, 128), 1)
     scaling = math.log2(math.e) / math.sqrt(HD)
     trans = (((1,), (1,)), ((), ()))
@@ -136,17 +147,32 @@
     key_other = lax.ppermute(key_maps, "core", swap)
     value_other = lax.ppermute(values, "core", swap)
 
-    spread = jnp.broadcast_to(queries.reshape(1, MAPS, HD), (COLUMN, MAPS, HD))
+    vmem = pl.BlockSpec(memory_space=pltpu.VMEM)
+    mask = pl.pallas_call(
+        causal_mask,
+        out_specs=vmem,
+        out_shape=jax.ShapeDtypeStruct((CHIPS, 2 * KEYS), F32),
+        compiler_params=pltpu.CompilerParams(vmem_limit_bytes=8 << 20),
+        cost_estimate=pl.CostEstimate(flops=1 << 31, bytes_accessed=1 << 18, transcendentals=0),
+        name="causal_mask",
+    )()
+    spread = pl.pallas_call(
+        own_row,
+        in_specs=[vmem, vmem],
+        out_specs=vmem,
+        out_shape=jax.ShapeDtypeStruct((COLUMN, MAPS, HD), BF16),
+        compiler_params=pltpu.CompilerParams(vmem_limit_bytes=8 << 20),
+        name="own_row",
+    )(queries, mask)
     column = lax.all_to_all(spread, ("z_lo", "z_hi"), 0, 0, tiled=True)
     column = column.reshape(COLUMN, MAPS * HD)
-    vmem = pl.BlockSpec(memory_space=pltpu.VMEM)
     spread = pl.pallas_call(
         repeat_rows,
         in_specs=[vmem],
         out_specs=vmem,
         out_shape=jax.ShapeDtypeStruct((CHIPS, MAPS * HD), BF16),
         compiler_params=pltpu.CompilerParams(vmem_limit_bytes=8 << 20),
-        cost_estimate=pl.CostEstimate(flops=1 << 34, bytes_accessed=1 << 20, transcendentals=0),
+        cost_estimate=pl.CostEstimate(flops=1 << 31, bytes_accessed=1 << 20, transcendentals=0),
         name="repeat_rows",
     )(column)
     spread = spread.reshape(PLANE, COLUMN, MAPS * HD)
@@ -154,13 +180,12 @@
 
     partial = pl.pallas_call(
         attend,
-        in_specs=[vmem] * 5,
+        in_specs=[vmem] * 6,
         out_specs=vmem,
         out_shape=jax.ShapeDtypeStruct((CHIPS, WIDE), BF16),
-        scratch_shapes=[pltpu.VMEM((CHIPS, 2 * KEYS), F32)],
         compiler_params=pltpu.CompilerParams(vmem_limit_bytes=16 << 20),
         name="attend",
-    )(q_all, key_maps, key_other, values, value_other)
+    )(q_all, key_maps, key_other, values, value_other, mask)
 
     partial = partial.reshape(PLANE, COLUMN, WIDE)
     partial = lax.all_to_all(partial, ("x", "y"), 0, 0, tiled=True)

time: 66.1 us -> 65.4 us (0.989)
  blocking collectives: 46 us -> 61.1 us
  starting transfers between devices: 9.08 us -> 0.51 us
  waiting for transfers between devices: 6.06 us -> 0.01 us
  other arithmetic: 0.73 us -> 0 us
    all_to_all x0 -> x1, blocking collectives: none -> 14.9 us  [shards(): column = lax.all_to_all(spread, ('z_lo', 'z_hi'), 0, 0, tiled=True)]
    all_to_all x1 -> x0, starting transfers between devices: 8.57 us -> none  [shards(): column = lax.all_to_all(spread, ('z_lo', 'z_hi'), 0, 0, tiled=True)]
    all_to_all x1 -> x0, waiting for transfers between devices: 6.05 us -> none  [shards(): column = lax.all_to_all(spread, ('z_lo', 'z_hi'), 0, 0, tiled=True)]
    unnamed x1 -> x0, other arithmetic: 0.73 us -> none
    pallas_call x1 -> x3, Pallas kernels: 1.85 us -> 1.91 us  [the longest x1 1.83 us: shards(): pl.pallas_call(attend, in_specs=[vmem] * 6, out_specs=vmem, out_shape=jax...]
  transfers between devices with their start and end apart: 3 -> 2, of which waited for: 1 -> 0; matrix products, arithmetic and copies ran while one was open for 0% -> 0% of each run, Pallas kernels for 0% -> 0%
where the time goes in v5:
time: 65.4 us; the launch traced here: 65.1 us
  blocking collectives  61.1 us (93%)
  Pallas kernels  3.26 us (5%)
    all_to_all x1, blocking collectives, shards(): partial = lax.all_to_all(partial, ('x', 'y'), 0, 0, tiled=True)  18.4 us
    all_to_all x1, blocking collectives, shards(): lax.all_to_all(spread, ('x', 'y'), 0, 0, tiled=True)  17.2 us
    all_to_all x1, blocking collectives, shards(): column = lax.all_to_all(spread, ('z_lo', 'z_hi'), 0, 0, tiled=True)  14.9 us
    all_to_all x1, blocking collectives, shards(): merged = lax.all_to_all(merged, ('z_lo', 'z_hi'), 0, 0, tiled=True)  10.6 us
    pallas_call x1, Pallas kernels, shards(): pl.pallas_call(attend, in_specs=[vmem] * 6, out_specs=vmem, out_shape=jax...  1.83 us
  transfers between devices with their start and end apart: 2, of which 0 were waited for; matrix products, arithmetic and copies ran while one was open for 0% of the time, Pallas kernels for 0%

profile of v5, /device:TPU:32, one launch (start us, length us, event | category | flops | bytes accessed | tf_op | source)
XLA Modules:
  0.0 65.1 jit_solution(15022000498483787931)
XLA Ops:
  0.0 0.0 copy-start.2
  0.0 0.0 collective-permute-start
  0.0 0.5 collective-permute-start.1
  0.5 0.1 causal_mask.1.mask_ref
  0.6 0.1 copy-done.2
  0.7 14.9 %all_to_all.20 = bf16[8,16,128]{2,1,0:T(8,128)(2,1)S(1)} all-to-all(bf16[8,16,128]{2,1,0:T(8,128)(2,1)S(1)} %own_row.1), channel_id=1, replica_groups=mesh['x'=4,'z_lo'=2,'y'=4,'z_hi'=4,'core'=2] {'z_lo','z_hi'}, dimensions={0} | all-to-all | bytes 65536 | tf_op jit(solution)/shard_map/all_to_all | solution.py:167
  15.7 0.0 copy-start.1
  15.7 0.0 copy-start
  15.7 17.2 %all_to_all.21 = bf16[16,8,2048]{2,1,0:T(8,128)(2,1)S(1)} all-to-all(bf16[16,8,2048]{2,1,0:T(8,128)(2,1)S(1)} %bitcast.15), channel_id=1, replica_groups=mesh['x'=4,'z_lo'=2,'y'=4,'z_hi'=4,'core'=2] {'x','y'}, dimensions={0} | all-to-all | bytes 1048576 | tf_op jit(solution)/shard_map/all_to_all | solution.py:179
  32.9 0.0 collective-permute-done.kb_ref
  32.9 0.0 collective-permute-done.1.vb_ref
  32.9 0.0 copy-done.1
  32.9 0.0 copy-done
  32.9 1.8 %attend.1 = bf16[128,4224]{1,0:T(8,128)(2,1)S(1)} custom-call(bf16[128,2048]{1,0:T(8,128)(2,1)S(1)} %bitcast.14, bf16[256,2048]{1,0:T(8,128)(2,1)S(1)} %copy-done, bf16[256,2048]{1,0:T(8,128)(2,1)S(1)} %collective-permute-done.kb_ref, bf16[256,2048]{1,0:T(8,128)(2,1)S(1)} %copy-done.1, bf16[256,2048]{1,0:T(8,128)(2,1)S(1)} %collective-permute-done.1.vb_ref, ...), custom_call_target="tpu_custom_call" | custom-call | tf_op jit(solution)/shard_map/attend/pallas_call | solution.py:181
  34.8 18.4 %all_to_all.22 = bf16[16,8,4224]{2,1,0:T(8,128)(2,1)S(1)} all-to-all(bf16[16,8,4224]{2,1,0:T(8,128)(2,1)S(1)} %bitcast.13), channel_id=1, replica_groups=mesh['x'=4,'z_lo'=2,'y'=4,'z_hi'=4,'core'=2] {'x','y'}, dimensions={0} | all-to-all | bytes 2162688 | tf_op jit(solution)/shard_map/all_to_all | solution.py:191
  53.2 0.0 copy-start.3
  53.2 0.0 copy-start.4
  53.2 0.4 merge_plane.1
  53.6 10.6 %all_to_all.23 = bf16[8,40,128]{2,1,0:T(8,128)(2,1)S(1)} all-to-all(bf16[8,40,128]{2,1,0:T(8,128)(2,1)S(1)} %bitcast.16), channel_id=1, replica_groups=mesh['x'=4,'z_lo'=2,'y'=4,'z_hi'=4,'core'=2] {'z_lo','z_hi'}, dimensions={0} | all-to-all | bytes 163840 | tf_op jit(solution)/shard_map/all_to_all | solution.py:202
  64.2 0.0 copy-done.3
  64.2 0.0 copy-done.4
  64.2 0.9 %merge_column.1 = bf16[1,2048]{1,0:T(2,128)(2,1)} custom-call(f32[1,8]{1,0:T(1,128)S(1)} %bitcast.20, bf16[320,128]{1,0:T(8,128)(2,1)S(1)} %bitcast.17, f32[1,2048]{1,0:T(1,128)S(1)} %bitcast.19), custom_call_target="tpu_custom_call" | custom-call | tf_op jit(solution)/shard_map/merge_column/pallas_call | solution.py:203
  (3 shorter events, 0.1 us)
Async XLA Ops:
  0.0 0.7 %copy-start.2 = (bf16[1,2048]{1,0:T(2,128)(2,1)S(1)}, bf16[1,2048]{1,0:T(2,128)(2,1)}, u32[]{:S(2)}) copy-start(bf16[1,2048]{1,0:T(2,128)(2,1)} %in_ref.1) | copy-start | bytes 12292
  0.0 32.9 %collective-permute-start = (bf16[256,2048]{1,0:T(8,128)(2,1)}, bf16[256,2048]{1,0:T(8,128)(2,1)S(1)}, u32[]{:S(2)}, u32[]{:S(2)}) collective-permute-start(bf16[256,2048]{1,0:T(8,128)(2,1)} %ka_ref.1), channel_id=1, source_target_pairs={{0,1},{1,0},{2,3},{3,2},{4,5},{5,4},{6,7},{7,6},{8,9},{9,8},{10,11... | collective-permute-start | bytes 3145736 | tf_op jit(solution)/shard_map/ppermute | solution.py:147
  0.0 32.9 %collective-permute-start.1 = (bf16[256,2048]{1,0:T(8,128)(2,1)}, bf16[256,2048]{1,0:T(8,128)(2,1)S(1)}, u32[]{:S(2)}, u32[]{:S(2)}) collective-permute-start(bf16[256,2048]{1,0:T(8,128)(2,1)} %va_ref.1), channel_id=1, source_target_pairs={{0,1},{1,0},{2,3},{3,2},{4,5},{5,4},{6,7},{7,6},{8,9},{9,8},{10,11... | collective-permute-start | bytes 3145736 | tf_op jit(solution)/shard_map/ppermute | solution.py:148
  15.7 17.3 %copy-start.1 = (bf16[256,2048]{1,0:T(8,128)(2,1)S(1)}, bf16[256,2048]{1,0:T(8,128)(2,1)}, u32[]{:S(2)}) copy-start(bf16[256,2048]{1,0:T(8,128)(2,1)} %va_ref.1) | copy-start | bytes 3145732
  15.7 17.2 %copy-start = (bf16[256,2048]{1,0:T(8,128)(2,1)S(1)}, bf16[256,2048]{1,0:T(8,128)(2,1)}, u32[]{:S(2)}) copy-start(bf16[256,2048]{1,0:T(8,128)(2,1)} %ka_ref.1) | copy-start | bytes 3145732
  53.2 11.1 %copy-start.3 = (f32[2048]{0:T(1024)S(1)}, f32[2048]{0:T(1024)}, u32[]{:S(2)}) copy-start(f32[2048]{0:T(1024)} %param.9) | copy-start | bytes 24580
  53.2 11.1 %copy-start.4 = (f32[8]{0:T(128)S(1)}, f32[8]{0:T(128)}, u32[]{:S(2)}) copy-start(f32[8]{0:T(128)} %param.8) | copy-start | bytes 100

commit v6 on v5

--- a/solution.py
+++ b/solution.py
@@ -21,22 +21,22 @@
 LINES = 40
 LAG = 3
 NEG = -1e30
-AXES = ("x", "z_lo", "y", "z_hi", "core")
+AXES = ("x1", "x0", "z0", "y1", "y0", "z2", "z1", "core")
+PLANE_AXES = ("x0", "y1", "x1", "y0")
+COLUMN_AXES = ("z0", "z1", "z2")
 BF16 = jnp.bfloat16
 F32 = jnp.float32
 
 
 def causal_mask(mask_ref):
     core = lax.axis_index("core")
-    place = (
-        lax.axis_index("x") * 64
-        + lax.axis_index("z_lo") * 32
-        + lax.axis_index("y") * 8
-        + lax.axis_index("z_hi") * 2
-        + core
-    )
+    place = core
     row = lax.broadcasted_iota(jnp.int32, (CHIPS, 1), 0)
-    device = (row // 32) * 64 + ((row // 4) % 2) * 32 + ((row // 8) % 4) * 8 + (row % 4) * 2 + core
+    device = row * 0 + core
+    for bit, axis in enumerate(reversed(PLANE_AXES + COLUMN_AXES)):
+        weight = 1 << (len(AXES) - 1 - AXES.index(axis))
+        place += lax.axis_index(axis) * weight
+        device += ((row >> bit) & 1) * weight
     last = device + (DEVICES - 1) * KEYS
     last_a = last - place * KEYS
     last_b = last - (place + 1 - 2 * core) * KEYS
@@ -164,7 +164,7 @@
         compiler_params=pltpu.CompilerParams(vmem_limit_bytes=8 << 20),
         name="own_row",
     )(queries, mask)
-    column = lax.all_to_all(spread, ("z_lo", "z_hi"), 0, 0, tiled=True)
+    column = lax.all_to_all(spread, COLUMN_AXES, 0, 0, tiled=True)
     column = column.reshape(COLUMN, MAPS * HD)
     spread = pl.pallas_call(
         repeat_rows,
@@ -176,7 +176,7 @@
         name="repeat_rows",
     )(column)
     spread = spread.reshape(PLANE, COLUMN, MAPS * HD)
-    q_all = lax.all_to_all(spread, ("x", "y"), 0, 0, tiled=True).reshape(CHIPS, MAPS * HD)
+    q_all = lax.all_to_all(spread, PLANE_AXES, 0, 0, tiled=True).reshape(CHIPS, MAPS * HD)
 
     partial = pl.pallas_call(
         attend,
@@ -188,7 +188,7 @@
     )(q_all, key_maps, key_other, values, value_other, mask)
 
     partial = partial.reshape(PLANE, COLUMN, WIDE)
-    partial = lax.all_to_all(partial, ("x", "y"), 0, 0, tiled=True)
+    partial = lax.all_to_all(partial, PLANE_AXES, 0, 0, tiled=True)
     merged = pl.pallas_call(
         merge_plane,
         in_specs=[vmem],
@@ -199,7 +199,7 @@
         name="merge_plane",
     )(partial.reshape(CHIPS, WIDE))
     merged = merged.reshape(COLUMN, LINES, 128)
-    merged = lax.all_to_all(merged, ("z_lo", "z_hi"), 0, 0, tiled=True)
+    merged = lax.all_to_all(merged, COLUMN_AXES, 0, 0, tiled=True)
     return pl.pallas_call(
         merge_column,
         in_specs=[vmem, vmem, vmem],
@@ -212,7 +212,7 @@
 
 
 def solution(mesh):
-    fine = Mesh(mesh.devices.reshape(4, 2, 4, 4, 2), AXES)
+    fine = Mesh(mesh.devices.reshape((2,) * len(AXES)), AXES)
     rows = P(AXES, None)
     return jax.shard_map(
         shards,

time: 65.4 us -> 65 us (level)
  no operation moved by 1% of the time
where the time goes in v6:
time: 65 us; the launch traced here: 64.6 us
  blocking collectives  60.6 us (93%)
  Pallas kernels  3.29 us (5%)
    all_to_all x1, blocking collectives, shards(): partial = lax.all_to_all(partial, PLANE_AXES, 0, 0, tiled=True)  18.3 us
    all_to_all x1, blocking collectives, shards(): lax.all_to_all(spread, PLANE_AXES, 0, 0, tiled=True)  17.2 us
    all_to_all x1, blocking collectives, shards(): column = lax.all_to_all(spread, COLUMN_AXES, 0, 0, tiled=True)  14.8 us
    all_to_all x1, blocking collectives, shards(): merged = lax.all_to_all(merged, COLUMN_AXES, 0, 0, tiled=True)  10.4 us
    pallas_call x1, Pallas kernels, shards(): pl.pallas_call(attend, in_specs=[vmem] * 6, out_specs=vmem, out_shape=jax...  1.83 us
  transfers between devices with their start and end apart: 2, of which 0 were waited for; matrix products, arithmetic and copies ran while one was open for 0% of the time, Pallas kernels for 0%

profile of v6, /device:TPU:32, one launch (start us, length us, event | category | flops | bytes accessed | tf_op | source)
XLA Modules:
  0.0 64.6 jit_solution(10510827461727998285)
XLA Ops:
  0.0 0.0 copy-start.2
  0.0 0.0 collective-permute-start
  0.0 0.5 collective-permute-start.1
  0.5 0.1 causal_mask.1.mask_ref
  0.6 0.1 copy-done.2
  0.7 14.8 %all_to_all.20 = bf16[8,16,128]{2,1,0:T(8,128)(2,1)S(1)} all-to-all(bf16[8,16,128]{2,1,0:T(8,128)(2,1)S(1)} %own_row.1), channel_id=1, replica_groups=mesh['x1'=2,'x0'=2,'z0'=2,'y1'=2,'y0'=2,'z2'=2,'z1'=2,'core'=2] {'z0','z..., dimensions={0} | all-to-all | bytes 65536 | tf_op jit(solution)/shard_map/all_to_all | solution.py:167
  15.5 0.0 copy-start.1
  15.6 0.0 copy-start
  15.6 17.2 %all_to_all.21 = bf16[16,8,2048]{2,1,0:T(8,128)(2,1)S(1)} all-to-all(bf16[16,8,2048]{2,1,0:T(8,128)(2,1)S(1)} %bitcast.15), channel_id=1, replica_groups=mesh['x1'=2,'x0'=2,'z0'=2,'y1'=2,'y0'=2,'z2'=2,'z1'=2,'core'=2] {'x0','y..., dimensions={0} | all-to-all | bytes 1048576 | tf_op jit(solution)/shard_map/all_to_all | solution.py:179
  32.8 0.0 collective-permute-done.kb_ref
  32.8 0.0 collective-permute-done.1.vb_ref
  32.8 0.0 copy-done.1
  32.8 0.0 copy-done
  32.8 1.8 %attend.1 = bf16[128,4224]{1,0:T(8,128)(2,1)S(1)} custom-call(bf16[128,2048]{1,0:T(8,128)(2,1)S(1)} %bitcast.14, bf16[256,2048]{1,0:T(8,128)(2,1)S(1)} %copy-done, bf16[256,2048]{1,0:T(8,128)(2,1)S(1)} %collective-permute-done.kb_ref, bf16[256,2048]{1,0:T(8,128)(2,1)S(1)} %copy-done.1, bf16[256,2048]{1,0:T(8,128)(2,1)S(1)} %collective-permute-done.1.vb_ref, ...), custom_call_target="tpu_custom_call" | custom-call | tf_op jit(solution)/shard_map/attend/pallas_call | solution.py:181
  34.6 18.3 %all_to_all.22 = bf16[16,8,4224]{2,1,0:T(8,128)(2,1)S(1)} all-to-all(bf16[16,8,4224]{2,1,0:T(8,128)(2,1)S(1)} %bitcast.13), channel_id=1, replica_groups=mesh['x1'=2,'x0'=2,'z0'=2,'y1'=2,'y0'=2,'z2'=2,'z1'=2,'core'=2] {'x0','y..., dimensions={0} | all-to-all | bytes 2162688 | tf_op jit(solution)/shard_map/all_to_all | solution.py:191
  52.9 0.0 copy-start.3
  52.9 0.0 copy-start.4
  52.9 0.4 merge_plane.1
  53.3 10.4 %all_to_all.23 = bf16[8,40,128]{2,1,0:T(8,128)(2,1)S(1)} all-to-all(bf16[8,40,128]{2,1,0:T(8,128)(2,1)S(1)} %bitcast.16), channel_id=1, replica_groups=mesh['x1'=2,'x0'=2,'z0'=2,'y1'=2,'y0'=2,'z2'=2,'z1'=2,'core'=2] {'z0','z..., dimensions={0} | all-to-all | bytes 163840 | tf_op jit(solution)/shard_map/all_to_all | solution.py:202
  63.7 0.0 copy-done.3
  63.7 0.0 copy-done.4
  63.7 0.9 %merge_column.1 = bf16[1,2048]{1,0:T(2,128)(2,1)} custom-call(f32[1,8]{1,0:T(1,128)S(1)} %bitcast.20, bf16[320,128]{1,0:T(8,128)(2,1)S(1)} %bitcast.17, f32[1,2048]{1,0:T(1,128)S(1)} %bitcast.19), custom_call_target="tpu_custom_call" | custom-call | tf_op jit(solution)/shard_map/merge_column/pallas_call | solution.py:203
  (3 shorter events, 0.1 us)
Async XLA Ops:
  0.0 0.7 %copy-start.2 = (bf16[1,2048]{1,0:T(2,128)(2,1)S(1)}, bf16[1,2048]{1,0:T(2,128)(2,1)}, u32[]{:S(2)}) copy-start(bf16[1,2048]{1,0:T(2,128)(2,1)} %in_ref.1) | copy-start | bytes 12292
  0.0 32.8 %collective-permute-start = (bf16[256,2048]{1,0:T(8,128)(2,1)}, bf16[256,2048]{1,0:T(8,128)(2,1)S(1)}, u32[]{:S(2)}, u32[]{:S(2)}) collective-permute-start(bf16[256,2048]{1,0:T(8,128)(2,1)} %ka_ref.1), channel_id=1, source_target_pairs={{0,1},{1,0},{2,3},{3,2},{4,5},{5,4},{6,7},{7,6},{8,9},{9,8},{10,11... | collective-permute-start | bytes 3145736 | tf_op jit(solution)/shard_map/ppermute | solution.py:147
  0.0 32.8 %collective-permute-start.1 = (bf16[256,2048]{1,0:T(8,128)(2,1)}, bf16[256,2048]{1,0:T(8,128)(2,1)S(1)}, u32[]{:S(2)}, u32[]{:S(2)}) collective-permute-start(bf16[256,2048]{1,0:T(8,128)(2,1)} %va_ref.1), channel_id=1, source_target_pairs={{0,1},{1,0},{2,3},{3,2},{4,5},{5,4},{6,7},{7,6},{8,9},{9,8},{10,11... | collective-permute-start | bytes 3145736 | tf_op jit(solution)/shard_map/ppermute | solution.py:148
  15.5 17.3 %copy-start.1 = (bf16[256,2048]{1,0:T(8,128)(2,1)S(1)}, bf16[256,2048]{1,0:T(8,128)(2,1)}, u32[]{:S(2)}) copy-start(bf16[256,2048]{1,0:T(8,128)(2,1)} %va_ref.1) | copy-start | bytes 3145732
  15.6 17.2 %copy-start = (bf16[256,2048]{1,0:T(8,128)(2,1)S(1)}, bf16[256,2048]{1,0:T(8,128)(2,1)}, u32[]{:S(2)}) copy-start(bf16[256,2048]{1,0:T(8,128)(2,1)} %ka_ref.1) | copy-start | bytes 3145732
  52.9 10.8 %copy-start.3 = (f32[2048]{0:T(1024)S(1)}, f32[2048]{0:T(1024)}, u32[]{:S(2)}) copy-start(f32[2048]{0:T(1024)} %param.9) | copy-start | bytes 24580
  52.9 10.8 %copy-start.4 = (f32[8]{0:T(128)S(1)}, f32[8]{0:T(128)}, u32[]{:S(2)}) copy-start(f32[8]{0:T(128)} %param.8) | copy-start | bytes 100

commit v7 on v6

--- a/solution.py
+++ b/solution.py
@@ -22,7 +22,7 @@
 LAG = 3
 NEG = -1e30
 AXES = ("x1", "x0", "z0", "y1", "y0", "z2", "z1", "core")
-PLANE_AXES = ("x0", "y1", "x1", "y0")
+PLANE_AXES = ("x0", "x1", "y1", "y0")
 COLUMN_AXES = ("z0", "z1", "z2")
 BF16 = jnp.bfloat16
 F32 = jnp.float32
@@ -55,9 +55,10 @@
 
 def repeat_rows(in_ref, out_ref):
     rows = in_ref[...].astype(F32)
-    rows = jnp.concatenate([rows, rows], axis=0).astype(BF16)
+    wide = jnp.concatenate([rows[:, index, :] for index in range(MAPS)], axis=1)
+    wide = jnp.concatenate([wide, wide], axis=0).astype(BF16)
     for start in range(0, CHIPS, 2 * COLUMN):
-        out_ref[start : start + 2 * COLUMN, :] = rows
+        out_ref[start : start + 2 * COLUMN, :] = wide
 
 
 def attend(q_ref, ka_ref, kb_ref, va_ref, vb_ref, mask_ref, out_ref):
@@ -165,7 +166,6 @@
         name="own_row",
     )(queries, mask)
     column = lax.all_to_all(spread, COLUMN_AXES, 0, 0, tiled=True)
-    column = column.reshape(COLUMN, MAPS * HD)
     spread = pl.pallas_call(
         repeat_rows,
         in_specs=[vmem],

time: 65 us -> 64.9 us (level)
  no operation moved by 1% of the time
where the time goes in v7:
time: 64.9 us; the launch traced here: 64.5 us
  blocking collectives  60.5 us (93%)
  Pallas kernels  3.3 us (5%)
    all_to_all x1, blocking collectives, shards(): partial = lax.all_to_all(partial, PLANE_AXES, 0, 0, tiled=True)  18.1 us
    all_to_all x1, blocking collectives, shards(): lax.all_to_all(spread, PLANE_AXES, 0, 0, tiled=True)  17.2 us
    all_to_all x1, blocking collectives, shards(): column = lax.all_to_all(spread, COLUMN_AXES, 0, 0, tiled=True)  14.8 us
    all_to_all x1, blocking collectives, shards(): merged = lax.all_to_all(merged, COLUMN_AXES, 0, 0, tiled=True)  10.5 us
    pallas_call x1, Pallas kernels, shards(): pl.pallas_call(attend, in_specs=[vmem] * 6, out_specs=vmem, out_shape=jax...  1.83 us
  transfers between devices with their start and end apart: 2, of which 0 were waited for; matrix products, arithmetic and copies ran while one was open for 0% of the time, Pallas kernels for 0%

profile of v7, /device:TPU:32, one launch (start us, length us, event | category | flops | bytes accessed | tf_op | source)
XLA Modules:
  0.0 64.5 jit_solution(16263905483070515038)
XLA Ops:
  0.0 0.0 copy-start.2
  0.0 0.0 collective-permute-start
  0.0 0.5 collective-permute-start.1
  0.5 0.1 causal_mask.1.mask_ref
  0.6 0.1 copy-done.2
  0.7 14.8 %all_to_all.20.in_ref = bf16[8,16,128]{2,1,0:T(8,128)(2,1)S(1)} all-to-all(bf16[8,16,128]{2,1,0:T(8,128)(2,1)S(1)} %own_row.1), channel_id=1, replica_groups=mesh['x1'=2,'x0'=2,'z0'=2,'y1'=2,'y0'=2,'z2'=2,'z1'=2,'core'=2] {'z0','z..., dimensions={0} | all-to-all | bytes 65536 | tf_op jit(solution)/shard_map/all_to_all | solution.py:168
  15.5 0.0 copy-start.1
  15.5 0.1 repeat_rows.1
  15.5 0.0 copy-start
  15.6 17.2 %all_to_all.21 = bf16[16,8,2048]{2,1,0:T(8,128)(2,1)S(1)} all-to-all(bf16[16,8,2048]{2,1,0:T(8,128)(2,1)S(1)} %bitcast.11), channel_id=1, replica_groups=mesh['x1'=2,'x0'=2,'z0'=2,'y1'=2,'y0'=2,'z2'=2,'z1'=2,'core'=2] {'x0','x..., dimensions={0} | all-to-all | bytes 1048576 | tf_op jit(solution)/shard_map/all_to_all | solution.py:179
  32.7 0.0 collective-permute-done.kb_ref
  32.7 0.0 collective-permute-done.1.vb_ref
  32.7 0.0 copy-done.1
  32.8 0.0 copy-done
  32.8 1.8 %attend.1 = bf16[128,4224]{1,0:T(8,128)(2,1)S(1)} custom-call(bf16[128,2048]{1,0:T(8,128)(2,1)S(1)} %bitcast.10, bf16[256,2048]{1,0:T(8,128)(2,1)S(1)} %copy-done, bf16[256,2048]{1,0:T(8,128)(2,1)S(1)} %collective-permute-done.kb_ref, bf16[256,2048]{1,0:T(8,128)(2,1)S(1)} %copy-done.1, bf16[256,2048]{1,0:T(8,128)(2,1)S(1)} %collective-permute-done.1.vb_ref, ...), custom_call_target="tpu_custom_call" | custom-call | tf_op jit(solution)/shard_map/attend/pallas_call | solution.py:181
  34.6 18.1 %all_to_all.22 = bf16[16,8,4224]{2,1,0:T(8,128)(2,1)S(1)} all-to-all(bf16[16,8,4224]{2,1,0:T(8,128)(2,1)S(1)} %bitcast.9), channel_id=1, replica_groups=mesh['x1'=2,'x0'=2,'z0'=2,'y1'=2,'y0'=2,'z2'=2,'z1'=2,'core'=2] {'x0','x..., dimensions={0} | all-to-all | bytes 2162688 | tf_op jit(solution)/shard_map/all_to_all | solution.py:191
  52.7 0.0 copy-start.3
  52.7 0.0 copy-start.4
  52.7 0.4 merge_plane.1
  53.1 10.5 %all_to_all.23 = bf16[8,40,128]{2,1,0:T(8,128)(2,1)S(1)} all-to-all(bf16[8,40,128]{2,1,0:T(8,128)(2,1)S(1)} %bitcast.12), channel_id=1, replica_groups=mesh['x1'=2,'x0'=2,'z0'=2,'y1'=2,'y0'=2,'z2'=2,'z1'=2,'core'=2] {'z0','z..., dimensions={0} | all-to-all | bytes 163840 | tf_op jit(solution)/shard_map/all_to_all | solution.py:202
  63.6 0.0 copy-done.3
  63.6 0.0 copy-done.4
  63.6 0.9 %merge_column.1 = bf16[1,2048]{1,0:T(2,128)(2,1)} custom-call(f32[1,8]{1,0:T(1,128)S(1)} %bitcast.15, bf16[320,128]{1,0:T(8,128)(2,1)S(1)} %bitcast.13, f32[1,2048]{1,0:T(1,128)S(1)} %bitcast.14), custom_call_target="tpu_custom_call" | custom-call | tf_op jit(solution)/shard_map/merge_column/pallas_call | solution.py:203
  (1 shorter events, 0.0 us)
Async XLA Ops:
  0.0 0.7 %copy-start.2 = (bf16[1,2048]{1,0:T(2,128)(2,1)S(1)}, bf16[1,2048]{1,0:T(2,128)(2,1)}, u32[]{:S(2)}) copy-start(bf16[1,2048]{1,0:T(2,128)(2,1)} %in_ref.1) | copy-start | bytes 12292
  0.0 32.7 %collective-permute-start = (bf16[256,2048]{1,0:T(8,128)(2,1)}, bf16[256,2048]{1,0:T(8,128)(2,1)S(1)}, u32[]{:S(2)}, u32[]{:S(2)}) collective-permute-start(bf16[256,2048]{1,0:T(8,128)(2,1)} %ka_ref.1), channel_id=1, source_target_pairs={{0,1},{1,0},{2,3},{3,2},{4,5},{5,4},{6,7},{7,6},{8,9},{9,8},{10,11... | collective-permute-start | bytes 3145736 | tf_op jit(solution)/shard_map/ppermute | solution.py:148
  0.0 32.7 %collective-permute-start.1 = (bf16[256,2048]{1,0:T(8,128)(2,1)}, bf16[256,2048]{1,0:T(8,128)(2,1)S(1)}, u32[]{:S(2)}, u32[]{:S(2)}) collective-permute-start(bf16[256,2048]{1,0:T(8,128)(2,1)} %va_ref.1), channel_id=1, source_target_pairs={{0,1},{1,0},{2,3},{3,2},{4,5},{5,4},{6,7},{7,6},{8,9},{9,8},{10,11... | collective-permute-start | bytes 3145736 | tf_op jit(solution)/shard_map/ppermute | solution.py:149
  15.5 17.3 %copy-start.1 = (bf16[256,2048]{1,0:T(8,128)(2,1)S(1)}, bf16[256,2048]{1,0:T(8,128)(2,1)}, u32[]{:S(2)}) copy-start(bf16[256,2048]{1,0:T(8,128)(2,1)} %va_ref.1) | copy-start | bytes 3145732
  15.5 17.2 %copy-start = (bf16[256,2048]{1,0:T(8,128)(2,1)S(1)}, bf16[256,2048]{1,0:T(8,128)(2,1)}, u32[]{:S(2)}) copy-start(bf16[256,2048]{1,0:T(8,128)(2,1)} %ka_ref.1) | copy-start | bytes 3145732
  52.7 10.9 %copy-start.3 = (f32[2048]{0:T(1024)S(1)}, f32[2048]{0:T(1024)}, u32[]{:S(2)}) copy-start(f32[2048]{0:T(1024)} %param.9) | copy-start | bytes 24580
  52.7 10.9 %copy-start.4 = (f32[8]{0:T(128)S(1)}, f32[8]{0:T(128)}, u32[]{:S(2)}) copy-start(f32[8]{0:T(128)} %param.8) | copy-start | bytes 100

commit v8 on v7

--- a/solution.py
+++ b/solution.py
@@ -75,7 +75,9 @@
             sb = lax.dot_general(q, kb_ref[:, cols], trans, preferred_element_type=F32) * scaling
             sa = sa + mask_ref[:, :KEYS]
             sb = sb + mask_ref[:, KEYS:]
-            top = jnp.max(jnp.maximum(sa, sb), axis=1, keepdims=True).astype(BF16).astype(F32)
+            wide = jnp.maximum(sa, sb)
+            wide = jnp.maximum(wide[:, :HD], wide[:, HD:]).astype(BF16)
+            top = jnp.max(wide, axis=1, keepdims=True).astype(F32)
             ea = jnp.exp2(sa - top)
             eb = jnp.exp2(sb - top)
             total = jnp.sum(ea + eb, axis=1, keepdims=True)

time: 64.9 us -> 64.9 us (level)
  no operation moved by 1% of the time
where the time goes in v8:
time: 64.9 us; the launch traced here: 64.5 us
  blocking collectives  60.5 us (93%)
  Pallas kernels  3.27 us (5%)
    all_to_all x1, blocking collectives, shards(): partial = lax.all_to_all(partial, PLANE_AXES, 0, 0, tiled=True)  18.1 us
    all_to_all x1, blocking collectives, shards(): lax.all_to_all(spread, PLANE_AXES, 0, 0, tiled=True)  17.2 us
    all_to_all x1, blocking collectives, shards(): column = lax.all_to_all(spread, COLUMN_AXES, 0, 0, tiled=True)  14.8 us
    all_to_all x1, blocking collectives, shards(): merged = lax.all_to_all(merged, COLUMN_AXES, 0, 0, tiled=True)  10.5 us
    pallas_call x1, Pallas kernels, shards(): pl.pallas_call(attend, in_specs=[vmem] * 6, out_specs=vmem, out_shape=jax...  1.81 us
  transfers between devices with their start and end apart: 2, of which 0 were waited for; matrix products, arithmetic and copies ran while one was open for 0% of the time, Pallas kernels for 0%

profile of v8, /device:TPU:32, one launch (start us, length us, event | category | flops | bytes accessed | tf_op | source)
XLA Modules:
  0.0 64.5 jit_solution(5684788421238854027)
XLA Ops:
  0.0 0.0 copy-start.2
  0.0 0.0 collective-permute-start
  0.0 0.5 collective-permute-start.1
  0.5 0.1 causal_mask.1.mask_ref
  0.6 0.1 copy-done.2
  0.7 14.8 %all_to_all.20.in_ref = bf16[8,16,128]{2,1,0:T(8,128)(2,1)S(1)} all-to-all(bf16[8,16,128]{2,1,0:T(8,128)(2,1)S(1)} %own_row.1), channel_id=1, replica_groups=mesh['x1'=2,'x0'=2,'z0'=2,'y1'=2,'y0'=2,'z2'=2,'z1'=2,'core'=2] {'z0','z..., dimensions={0} | all-to-all | bytes 65536 | tf_op jit(solution)/shard_map/all_to_all | solution.py:170
  15.5 0.0 copy-start.1
  15.5 0.1 repeat_rows.1
  15.5 0.0 copy-start
  15.6 17.2 %all_to_all.21 = bf16[16,8,2048]{2,1,0:T(8,128)(2,1)S(1)} all-to-all(bf16[16,8,2048]{2,1,0:T(8,128)(2,1)S(1)} %bitcast.11), channel_id=1, replica_groups=mesh['x1'=2,'x0'=2,'z0'=2,'y1'=2,'y0'=2,'z2'=2,'z1'=2,'core'=2] {'x0','x..., dimensions={0} | all-to-all | bytes 1048576 | tf_op jit(solution)/shard_map/all_to_all | solution.py:181
  32.7 0.0 collective-permute-done.kb_ref
  32.7 0.0 collective-permute-done.1.vb_ref
  32.7 0.0 copy-done.1
  32.8 0.0 copy-done
  32.8 1.8 %attend.1 = bf16[128,4224]{1,0:T(8,128)(2,1)S(1)} custom-call(bf16[128,2048]{1,0:T(8,128)(2,1)S(1)} %bitcast.10, bf16[256,2048]{1,0:T(8,128)(2,1)S(1)} %copy-done, bf16[256,2048]{1,0:T(8,128)(2,1)S(1)} %collective-permute-done.kb_ref, bf16[256,2048]{1,0:T(8,128)(2,1)S(1)} %copy-done.1, bf16[256,2048]{1,0:T(8,128)(2,1)S(1)} %collective-permute-done.1.vb_ref, ...), custom_call_target="tpu_custom_call" | custom-call | tf_op jit(solution)/shard_map/attend/pallas_call | solution.py:183
  34.6 18.1 %all_to_all.22 = bf16[16,8,4224]{2,1,0:T(8,128)(2,1)S(1)} all-to-all(bf16[16,8,4224]{2,1,0:T(8,128)(2,1)S(1)} %bitcast.9), channel_id=1, replica_groups=mesh['x1'=2,'x0'=2,'z0'=2,'y1'=2,'y0'=2,'z2'=2,'z1'=2,'core'=2] {'x0','x..., dimensions={0} | all-to-all | bytes 2162688 | tf_op jit(solution)/shard_map/all_to_all | solution.py:193
  52.6 0.0 copy-start.3
  52.7 0.0 copy-start.4
  52.7 0.4 merge_plane.1
  53.1 10.5 %all_to_all.23 = bf16[8,40,128]{2,1,0:T(8,128)(2,1)S(1)} all-to-all(bf16[8,40,128]{2,1,0:T(8,128)(2,1)S(1)} %bitcast.12), channel_id=1, replica_groups=mesh['x1'=2,'x0'=2,'z0'=2,'y1'=2,'y0'=2,'z2'=2,'z1'=2,'core'=2] {'z0','z..., dimensions={0} | all-to-all | bytes 163840 | tf_op jit(solution)/shard_map/all_to_all | solution.py:204
  63.6 0.0 copy-done.3
  63.6 0.0 copy-done.4
  63.6 0.9 %merge_column.1 = bf16[1,2048]{1,0:T(2,128)(2,1)} custom-call(f32[1,8]{1,0:T(1,128)S(1)} %bitcast.15, bf16[320,128]{1,0:T(8,128)(2,1)S(1)} %bitcast.13, f32[1,2048]{1,0:T(1,128)S(1)} %bitcast.14), custom_call_target="tpu_custom_call" | custom-call | tf_op jit(solution)/shard_map/merge_column/pallas_call | solution.py:205
  (1 shorter events, 0.0 us)
Async XLA Ops:
  0.0 0.7 %copy-start.2 = (bf16[1,2048]{1,0:T(2,128)(2,1)S(1)}, bf16[1,2048]{1,0:T(2,128)(2,1)}, u32[]{:S(2)}) copy-start(bf16[1,2048]{1,0:T(2,128)(2,1)} %in_ref.1) | copy-start | bytes 12292
  0.0 32.7 %collective-permute-start = (bf16[256,2048]{1,0:T(8,128)(2,1)}, bf16[256,2048]{1,0:T(8,128)(2,1)S(1)}, u32[]{:S(2)}, u32[]{:S(2)}) collective-permute-start(bf16[256,2048]{1,0:T(8,128)(2,1)} %ka_ref.1), channel_id=1, source_target_pairs={{0,1},{1,0},{2,3},{3,2},{4,5},{5,4},{6,7},{7,6},{8,9},{9,8},{10,11... | collective-permute-start | bytes 3145736 | tf_op jit(solution)/shard_map/ppermute | solution.py:150
  0.0 32.7 %collective-permute-start.1 = (bf16[256,2048]{1,0:T(8,128)(2,1)}, bf16[256,2048]{1,0:T(8,128)(2,1)S(1)}, u32[]{:S(2)}, u32[]{:S(2)}) collective-permute-start(bf16[256,2048]{1,0:T(8,128)(2,1)} %va_ref.1), channel_id=1, source_target_pairs={{0,1},{1,0},{2,3},{3,2},{4,5},{5,4},{6,7},{7,6},{8,9},{9,8},{10,11... | collective-permute-start | bytes 3145736 | tf_op jit(solution)/shard_map/ppermute | solution.py:151
  15.5 17.3 %copy-start.1 = (bf16[256,2048]{1,0:T(8,128)(2,1)S(1)}, bf16[256,2048]{1,0:T(8,128)(2,1)}, u32[]{:S(2)}) copy-start(bf16[256,2048]{1,0:T(8,128)(2,1)} %va_ref.1) | copy-start | bytes 3145732
  15.5 17.2 %copy-start = (bf16[256,2048]{1,0:T(8,128)(2,1)S(1)}, bf16[256,2048]{1,0:T(8,128)(2,1)}, u32[]{:S(2)}) copy-start(bf16[256,2048]{1,0:T(8,128)(2,1)} %ka_ref.1) | copy-start | bytes 3145732
  52.6 10.9 %copy-start.3 = (f32[2048]{0:T(1024)S(1)}, f32[2048]{0:T(1024)}, u32[]{:S(2)}) copy-start(f32[2048]{0:T(1024)} %param.9) | copy-start | bytes 24580
  52.7 10.9 %copy-start.4 = (f32[8]{0:T(128)S(1)}, f32[8]{0:T(128)}, u32[]{:S(2)}) copy-start(f32[8]{0:T(128)} %param.8) | copy-start | bytes 100

commit v9 on v8

--- a/solution.py
+++ b/solution.py
@@ -19,7 +19,7 @@
 SUMS = MAPS * VD
 WIDE = SUMS + 128
 LINES = 40
-LAG = 3
+LAG = 5
 NEG = -1e30
 AXES = ("x1", "x0", "z0", "y1", "y0", "z2", "z1", "core")
 PLANE_AXES = ("x0", "x1", "y1", "y0")

time: 64.9 us -> 64.9 us (level)
  no operation moved by 1% of the time
where the time goes in v9:
time: 64.9 us; the launch traced here: 64.5 us
  blocking collectives  60.5 us (93%)
  Pallas kernels  3.27 us (5%)
    all_to_all x1, blocking collectives, shards(): partial = lax.all_to_all(partial, PLANE_AXES, 0, 0, tiled=True)  18.1 us
    all_to_all x1, blocking collectives, shards(): lax.all_to_all(spread, PLANE_AXES, 0, 0, tiled=True)  17.2 us
    all_to_all x1, blocking collectives, shards(): column = lax.all_to_all(spread, COLUMN_AXES, 0, 0, tiled=True)  14.8 us
    all_to_all x1, blocking collectives, shards(): merged = lax.all_to_all(merged, COLUMN_AXES, 0, 0, tiled=True)  10.5 us
    pallas_call x1, Pallas kernels, shards(): pl.pallas_call(attend, in_specs=[vmem] * 6, out_specs=vmem, out_shape=jax...  1.81 us
  transfers between devices with their start and end apart: 2, of which 0 were waited for; matrix products, arithmetic and copies ran while one was open for 0% of the time, Pallas kernels for 0%

profile of v9, /device:TPU:32, one launch (start us, length us, event | category | flops | bytes accessed | tf_op | source)
XLA Modules:
  0.0 64.5 jit_solution(4610022993106645553)
XLA Ops:
  0.0 0.0 copy-start.2
  0.0 0.0 collective-permute-start
  0.0 0.5 collective-permute-start.1
  0.5 0.1 causal_mask.1.mask_ref
  0.6 0.1 copy-done.2
  0.7 14.8 %all_to_all.20.in_ref = bf16[8,16,128]{2,1,0:T(8,128)(2,1)S(1)} all-to-all(bf16[8,16,128]{2,1,0:T(8,128)(2,1)S(1)} %own_row.1), channel_id=1, replica_groups=mesh['x1'=2,'x0'=2,'z0'=2,'y1'=2,'y0'=2,'z2'=2,'z1'=2,'core'=2] {'z0','z..., dimensions={0} | all-to-all | bytes 65536 | tf_op jit(solution)/shard_map/all_to_all | solution.py:170
  15.5 0.0 copy-start.1
  15.5 0.1 repeat_rows.1
  15.5 0.0 copy-start
  15.6 17.2 %all_to_all.21 = bf16[16,8,2048]{2,1,0:T(8,128)(2,1)S(1)} all-to-all(bf16[16,8,2048]{2,1,0:T(8,128)(2,1)S(1)} %bitcast.11), channel_id=1, replica_groups=mesh['x1'=2,'x0'=2,'z0'=2,'y1'=2,'y0'=2,'z2'=2,'z1'=2,'core'=2] {'x0','x..., dimensions={0} | all-to-all | bytes 1048576 | tf_op jit(solution)/shard_map/all_to_all | solution.py:181
  32.7 0.0 collective-permute-done.kb_ref
  32.7 0.0 collective-permute-done.1.vb_ref
  32.7 0.0 copy-done.1
  32.8 0.0 copy-done
  32.8 1.8 %attend.1 = bf16[128,4224]{1,0:T(8,128)(2,1)S(1)} custom-call(bf16[128,2048]{1,0:T(8,128)(2,1)S(1)} %bitcast.10, bf16[256,2048]{1,0:T(8,128)(2,1)S(1)} %copy-done, bf16[256,2048]{1,0:T(8,128)(2,1)S(1)} %collective-permute-done.kb_ref, bf16[256,2048]{1,0:T(8,128)(2,1)S(1)} %copy-done.1, bf16[256,2048]{1,0:T(8,128)(2,1)S(1)} %collective-permute-done.1.vb_ref, ...), custom_call_target="tpu_custom_call" | custom-call | tf_op jit(solution)/shard_map/attend/pallas_call | solution.py:183
  34.6 18.1 %all_to_all.22 = bf16[16,8,4224]{2,1,0:T(8,128)(2,1)S(1)} all-to-all(bf16[16,8,4224]{2,1,0:T(8,128)(2,1)S(1)} %bitcast.9), channel_id=1, replica_groups=mesh['x1'=2,'x0'=2,'z0'=2,'y1'=2,'y0'=2,'z2'=2,'z1'=2,'core'=2] {'x0','x..., dimensions={0} | all-to-all | bytes 2162688 | tf_op jit(solution)/shard_map/all_to_all | solution.py:193
  52.6 0.0 copy-start.3
  52.6 0.0 copy-start.4
  52.7 0.4 merge_plane.1
  53.1 10.5 %all_to_all.23 = bf16[8,40,128]{2,1,0:T(8,128)(2,1)S(1)} all-to-all(bf16[8,40,128]{2,1,0:T(8,128)(2,1)S(1)} %bitcast.12), channel_id=1, replica_groups=mesh['x1'=2,'x0'=2,'z0'=2,'y1'=2,'y0'=2,'z2'=2,'z1'=2,'core'=2] {'z0','z..., dimensions={0} | all-to-all | bytes 163840 | tf_op jit(solution)/shard_map/all_to_all | solution.py:204
  63.6 0.0 copy-done.3
  63.6 0.0 copy-done.4
  63.6 0.9 %merge_column.1 = bf16[1,2048]{1,0:T(2,128)(2,1)} custom-call(f32[1,8]{1,0:T(1,128)S(1)} %bitcast.15, bf16[320,128]{1,0:T(8,128)(2,1)S(1)} %bitcast.13, f32[1,2048]{1,0:T(1,128)S(1)} %bitcast.14), custom_call_target="tpu_custom_call" | custom-call | tf_op jit(solution)/shard_map/merge_column/pallas_call | solution.py:205
  (1 shorter events, 0.0 us)
Async XLA Ops:
  0.0 0.7 %copy-start.2 = (bf16[1,2048]{1,0:T(2,128)(2,1)S(1)}, bf16[1,2048]{1,0:T(2,128)(2,1)}, u32[]{:S(2)}) copy-start(bf16[1,2048]{1,0:T(2,128)(2,1)} %in_ref.1) | copy-start | bytes 12292
  0.0 32.7 %collective-permute-start = (bf16[256,2048]{1,0:T(8,128)(2,1)}, bf16[256,2048]{1,0:T(8,128)(2,1)S(1)}, u32[]{:S(2)}, u32[]{:S(2)}) collective-permute-start(bf16[256,2048]{1,0:T(8,128)(2,1)} %ka_ref.1), channel_id=1, source_target_pairs={{0,1},{1,0},{2,3},{3,2},{4,5},{5,4},{6,7},{7,6},{8,9},{9,8},{10,11... | collective-permute-start | bytes 3145736 | tf_op jit(solution)/shard_map/ppermute | solution.py:150
  0.0 32.7 %collective-permute-start.1 = (bf16[256,2048]{1,0:T(8,128)(2,1)}, bf16[256,2048]{1,0:T(8,128)(2,1)S(1)}, u32[]{:S(2)}, u32[]{:S(2)}) collective-permute-start(bf16[256,2048]{1,0:T(8,128)(2,1)} %va_ref.1), channel_id=1, source_target_pairs={{0,1},{1,0},{2,3},{3,2},{4,5},{5,4},{6,7},{7,6},{8,9},{9,8},{10,11... | collective-permute-start | bytes 3145736 | tf_op jit(solution)/shard_map/ppermute | solution.py:151
  15.5 17.3 %copy-start.1 = (bf16[256,2048]{1,0:T(8,128)(2,1)S(1)}, bf16[256,2048]{1,0:T(8,128)(2,1)}, u32[]{:S(2)}) copy-start(bf16[256,2048]{1,0:T(8,128)(2,1)} %va_ref.1) | copy-start | bytes 3145732
  15.5 17.2 %copy-start = (bf16[256,2048]{1,0:T(8,128)(2,1)S(1)}, bf16[256,2048]{1,0:T(8,128)(2,1)}, u32[]{:S(2)}) copy-start(bf16[256,2048]{1,0:T(8,128)(2,1)} %ka_ref.1) | copy-start | bytes 3145732
  52.6 10.9 %copy-start.3 = (f32[2048]{0:T(1024)S(1)}, f32[2048]{0:T(1024)}, u32[]{:S(2)}) copy-start(f32[2048]{0:T(1024)} %param.9) | copy-start | bytes 24580
  52.6 10.9 %copy-start.4 = (f32[8]{0:T(128)S(1)}, f32[8]{0:T(128)}, u32[]{:S(2)}) copy-start(f32[8]{0:T(128)} %param.8) | copy-start | bytes 100
